TPU v7x, 32 devices: a whole 2x2x4 slice. The times are simulated.
32 devices in a mesh: row: 8 (over z, x), col: 4 (over y, core).
Axes of the slice: x: 2, y: 2, z: 4, core: 2. Of those that a mesh axis runs over, the one named last changes fastest.
Arguments:
- positions: float32 [3, 8192], P(None, ('row', 'col')), may hold values from 0 to 64, as said below
- forces: float32 [3, 8192], P(None, ('row', 'col')), may hold values from -6 to 6
Outputs:
- velocities: float32 [3, 8192], P(None, ('row', 'col'))
Inputs may be any that keep to these rules, and one draw needn't show every extreme that they name: `positions`: the first two coordinates lie within 0 to 64, the third within 0 to 51.
All inputs are finite; a program needn't handle non-finite values.
Results may differ from a plain program's by a relative error of at most 0.0003.
Values sent between devices are 32-bit elements; how exact they have to be, the bound alone decides.
No kernel may reach another device: no remote copies, remote signals or barrier semaphores. Data moves between devices by JAX's collectives and lax.ppermute only.
A program may use at most 64 MiB of HBM per device.

v0:
```python
import math

import jax
import jax.numpy as jnp
from jax import lax
from jax.sharding import PartitionSpec as P

mobility_scale = 0.25


def tensor_parts(target_pos, source_pos):
    offset = target_pos[:, :, None] - source_pos[:, None, :]
    squared = jnp.sum(offset * offset, axis=0)
    inverse = lax.rsqrt(jnp.maximum(squared, 1e-12))
    distance = squared * inverse
    near = distance < 2.0
    cubed = inverse * inverse * inverse
    scalar_part = jnp.where(near, 1.0 - 9.0 / 32.0 * distance, 0.75 * inverse + 0.5 * cubed)
    dyad_part = jnp.where(
        near, 3.0 / 32.0 * inverse, (0.75 * inverse - 1.5 * cubed) * inverse * inverse
    )
    return (offset, scalar_part, dyad_part)


def pair_sum(target_pos, source_pos, source_frc):
    offset, scalar_part, dyad_part = tensor_parts(target_pos, source_pos)
    projected = jnp.sum(offset * source_frc[:, None, :], axis=0)
    terms = scalar_part[None] * source_frc[:, None, :] + (dyad_part * projected)[None] * offset
    return jnp.sum(terms, axis=2)


def make_fold(targets, pieces):
    target_count = targets.shape[1]
    tile_width = math.gcd(target_count, 256)
    tile_count = target_count // tile_width
    target_tiles = targets.reshape(3, tile_count, tile_width).transpose(1, 0, 2)
    source_pos, source_frc = pieces
    source_count = source_pos.shape[1]
    width = math.gcd(source_count, 512)
    blocks = source_count // width
    stacked_pos = source_pos.reshape(3, blocks, width).transpose(1, 0, 2)
    stacked_frc = source_frc.reshape(3, blocks, width).transpose(1, 0, 2)

    def per_tile(tile_pos):

        def step(total, source_block):
            return (total + pair_sum(tile_pos, source_block[0], source_block[1]), None)

        total, _ = lax.scan(
            step, jnp.zeros((3, tile_width), jnp.float32), (stacked_pos, stacked_frc)
        )
        return total

    added = lax.map(per_tile, target_tiles)
    return added.transpose(1, 0, 2).reshape(3, target_count)


def body(positions, forces):
    total = make_fold(
        positions,
        (
            lax.all_gather(positions, ("row", "col"), axis=1, tiled=True),
            lax.all_gather(forces, ("row", "col"), axis=1, tiled=True),
        ),
    )
    return total * mobility_scale


def solution(mesh):
    return jax.shard_map(
        body,
        mesh=mesh,
        in_specs=(P(None, ("row", "col")), P(None, ("row", "col"))),
        out_specs=P(None, ("row", "col")),
        check_vma=False,
    )
```

profile of v0, /device:TPU:0, one launch (start us, length us, event | category | flops | bytes accessed | tf_op | source)
XLA Modules:
  0.0 118.2 jit_solution(17376268508990252791)
XLA Ops:
  0.0 43.8 %all_gather.6 = f32[3,8192]{1,0:T(4,128)S(1)} all-gather(f32[3,256]{1,0:T(4,128)} %param.4), channel_id=1, replica_groups=mesh['row'=8,'col'=4] {'row','col'}, dimensions={1}, use_global_device_ids=true | all-gather | bytes 101376 | tf_op jit(solution)/shard_map/all_gather | solution.py:62
  43.8 37.2 %all_gather.7 = f32[3,8192]{1,0:T(4,128)S(1)} all-gather(f32[3,256]{1,0:T(4,128)} %param.5), channel_id=1, replica_groups=mesh['row'=8,'col'=4] {'row','col'}, dimensions={1}, use_global_device_ids=true | all-gather | bytes 101376 | tf_op jit(solution)/shard_map/all_gather | solution.py:63
  81.0 36.6 %while.18 = (s32[]{:T(128)}, f32[3,256]{1,0:T(4,128)S(1)}, f32[3,256]{1,0:T(4,128)}, f32[16,3,512]{2,1,0:T(4,128)S(1)}, f32[16,3,512]{2,1,0:T(4,128)S(1)}, /*index=5*/s32[]{:T(128)}, s32[]{:T(128)}) while((s32[]{:T(128)}, f32[3,256]{1,0:T(4,128)S(1)}, f32[3,256]{1,0:T(4,128)}, f32[16,3,512]{2,1,0:T(4,128)S(1)}, ...), condition=%wide.region_4.5_spmd.clone, body=%wide.region_0.4_spmd.clone.sunk | while | flops 6030083 | bytes 4274295 | solution.py:49
  81.1 1.1 fusion.10
  82.2 0.4 add_select_fusion.2
  82.5 0.3 copy-done
  82.9 0.4 fusion.11
  83.3 1.1 fusion.10
  84.5 0.4 add_select_fusion.2
  85.1 0.4 fusion.11
  85.6 1.1 fusion.10
  86.7 0.4 add_select_fusion.2
  87.1 0.3 copy-done
  87.4 0.4 fusion.11
  87.9 1.1 fusion.10
  89.0 0.4 add_select_fusion.2
  89.4 0.3 copy-done
  89.7 0.4 fusion.11
  90.2 1.1 fusion.10
  91.3 0.4 add_select_fusion.2
  91.7 0.3 copy-done
  92.0 0.4 fusion.11
  92.5 1.1 fusion.10
  93.6 0.4 add_select_fusion.2
  94.0 0.3 copy-done
  94.3 0.4 fusion.11
  94.8 1.1 fusion.10
  95.9 0.4 add_select_fusion.2
  96.3 0.3 copy-done
  96.6 0.4 fusion.11
  97.1 1.1 fusion.10
  98.2 0.4 add_select_fusion.2
  98.5 0.3 copy-done
  98.9 0.4 fusion.11
  99.3 1.1 fusion.10
  100.5 0.4 add_select_fusion.2
  100.8 0.3 copy-done
  101.1 0.4 fusion.11
  101.6 1.1 fusion.10
  102.8 0.4 add_select_fusion.2
  103.1 0.3 copy-done
  103.4 0.4 fusion.11
  103.9 1.1 fusion.10
  105.0 0.4 add_select_fusion.2
  105.7 0.4 fusion.11
  106.2 1.1 fusion.10
  107.3 0.4 add_select_fusion.2
  107.7 0.3 copy-done
  108.0 0.4 fusion.11
  108.5 1.1 fusion.10
  109.6 0.4 add_select_fusion.2
  110.0 0.3 copy-done
  110.3 0.4 fusion.11
  110.8 1.1 fusion.10
  111.9 0.4 add_select_fusion.2
  112.3 0.3 copy-done
  112.6 0.4 fusion.11
  113.1 1.1 fusion.10
  114.2 0.4 add_select_fusion.2
  114.9 0.4 fusion.11
  115.4 1.1 fusion.10
  116.5 0.4 add_select_fusion.2
  117.2 0.4 fusion.11
  117.6 0.6 broadcast_multiply_fusion
  (53 shorter events, 1.7 us)
Async XLA Ops:
  82.2 0.7 copy-start
  84.4 0.7 copy-start
  86.7 0.7 copy-start
  89.0 0.7 copy-start
  91.3 0.7 copy-start
  93.6 0.7 copy-start
  95.9 0.7 copy-start
  98.2 0.7 copy-start
  100.5 0.7 copy-start
  102.7 0.7 copy-start
  105.0 0.7 copy-start
  107.3 0.7 copy-start
  109.6 0.7 copy-start
  111.9 0.7 copy-start
  114.2 0.7 copy-start
  116.5 0.7 copy-start
where the time goes:
time: 119 us; the launch traced here: 118 us
  blocking collectives  81 us (68%)
  other arithmetic  31.2 us (26%)
  local copies, waits for them, and re-layouts  5.23 us (4%)
    all_gather x1, blocking collectives, body(): lax.all_gather(positions, ('row', 'col'), axis=1, tiled=True)  43.8 us
    all_gather x1, blocking collectives, body(): lax.all_gather(forces, ('row', 'col'), axis=1, tiled=True)  37.2 us
    reduce_sum x16, other arithmetic, tensor_parts(): squared = jnp.sum(offset * offset, axis=0)  17.6 us
    reduce_sum x16, other arithmetic, pair_sum(): return jnp.sum(terms, axis=2)  7.02 us
    select_n x16, other arithmetic, tensor_parts(): jnp.where(near, 1.0 - 9.0 / 32.0 * distance, 0.75 * inverse + 0.5 * cubed)  5.73 us
    while x32, local copies, waits for them, and re-layouts  5.08 us

commit v1 on v0

v1 whole, which is shorter than its diff:
```python
import functools

import jax
import jax.numpy as jnp
from jax import lax
from jax.experimental import pallas as pl
from jax.experimental.pallas import tpu as pltpu
from jax.sharding import PartitionSpec as P

f32 = jnp.float32
AXES = ("row", "col")
LANES = 128
GROUP = 32
VMEM = pl.BlockSpec(memory_space=pltpu.VMEM)


def pair_terms(target, source):
    dx, dy, dz = target[0] - source[0], target[1] - source[1], target[2] - source[2]
    squared = dx * dx + dy * dy + dz * dz
    inverse = lax.rsqrt(jnp.maximum(squared, 1e-12))
    capped = jnp.minimum(inverse, 0.5)
    q = capped * capped
    mixed = inverse * capped
    scalar = capped * (4.0 - (squared * mixed) * (2.5 - q))
    dyad = (mixed * capped) * (1.5 - 3.0 * q)
    w = dyad * (dx * source[3] + dy * source[4] + dz * source[5])
    return scalar * source[3] + w * dx, scalar * source[4] + w * dy, scalar * source[5] + w * dz


def kernel(count, first, last, tgt_ref, *refs):
    sources = refs[:count]
    prev_ref = None if first else refs[count]
    out_ref = refs[count + (not first)]
    acc_ref = refs[-1] if last else out_ref
    targets = tgt_ref.shape[1]
    columns = jnp.transpose(tgt_ref[...])

    for base in range(0, targets, GROUP):
        target = [
            jnp.broadcast_to(columns[base : base + GROUP, k : k + 1], (GROUP, LANES))
            for k in range(3)
        ]
        if first:
            acc = tuple(jnp.zeros((GROUP, LANES), f32) for _ in range(3))
        else:
            acc = tuple(prev_ref[k, base : base + GROUP, :] for k in range(3))
        for ref in sources:
            blocks, _, width = ref.shape

            def step(i, acc, ref=ref, width=width, target=target):
                for at in range(0, width, LANES):
                    source = [
                        jnp.broadcast_to(ref[i, k : k + 1, at : at + LANES], (GROUP, LANES))
                        for k in range(6)
                    ]
                    acc = tuple(a + t for a, t in zip(acc, pair_terms(target, source)))
                return acc

            acc = lax.fori_loop(0, blocks, step, acc, unroll=min(blocks, 4))
        for k in range(3):
            acc_ref[k, base : base + GROUP, :] = acc[k]
    if last:
        ones = jnp.full((8, LANES), 0.125, f32)
        for k in range(3):
            total = lax.dot_general(
                ones,
                acc_ref[k],
                (((1,), (1,)), ((), ())),
                precision=lax.Precision.HIGHEST,
                preferred_element_type=f32,
            )
            out_ref[k : k + 1, :] = total[0:1, :]


def accumulate(target, sources, prev, last):
    targets = target.shape[1]
    pairs = targets * sum(s.shape[0] * s.shape[2] for s in sources)
    acc_shape = (3, targets, LANES)
    args = [target, *sources] + ([] if prev is None else [prev])
    return pl.pallas_call(
        functools.partial(kernel, len(sources), prev is None, last),
        out_shape=jax.ShapeDtypeStruct((3, targets) if last else acc_shape, f32),
        in_specs=[VMEM] * len(args),
        out_specs=VMEM,
        scratch_shapes=[pltpu.VMEM(acc_shape, f32)] if last else [],
        cost_estimate=pl.CostEstimate(flops=38 * pairs, bytes_accessed=0, transcendentals=pairs),
    )(*args)


def body(sizes, positions, forces):
    devices = sizes[0] * sizes[1]

    def swap(block, bit):
        return lax.ppermute(block, AXES, [(i, i ^ bit) for i in range(devices)])

    bits = []
    bit = devices // 2
    while bit > 1:
        bits.append(bit)
        bit //= 2

    own = jnp.concatenate([positions, forces, jnp.zeros((2, positions.shape[1]), f32)], axis=0)
    target = own
    held = own[None]
    mine, theirs = [held], [swap(held, 1)]
    for bit in bits:
        got = swap(held, bit)
        mine.append(got)
        theirs.append(swap(got, 1))
        held = jnp.concatenate([held, got], axis=0)
    acc = accumulate(target, mine[:-2] + theirs[:-2], None, False)
    acc = accumulate(target, [mine[-2], theirs[-2]], acc, False)
    acc = accumulate(target, [mine[-1]], acc, False)
    return accumulate(target, [theirs[-1]], acc, True)


def solution(mesh):
    sizes = (mesh.shape["row"], mesh.shape["col"])
    return jax.shard_map(
        functools.partial(body, sizes),
        mesh=mesh,
        in_specs=(P(None, AXES), P(None, AXES)),
        out_specs=P(None, AXES),
        check_vma=False,
    )
```

time: 119 us -> 44 us (0.37)
  blocking collectives: 81 us -> 0 us
  other arithmetic: 31.2 us -> 0.78 us
  Pallas kernels: 0 us -> 20.5 us
  starting transfers between devices: 0 us -> 10.8 us
  waiting for transfers between devices: 0 us -> 9.08 us
  local copies, waits for them, and re-layouts: 5.23 us -> 2.51 us
    all_gather x2 -> x0, blocking collectives: 81 us -> none  [the longest x1 43.8 us: body(): lax.all_gather(positions, ('row', 'col'), axis=1, tiled=True)]
    reduce_sum x32 -> x0, other arithmetic: 24.7 us -> none  [the longest x16 17.6 us: tensor_parts(): squared = jnp.sum(offset * offset, axis=0)]
    pallas_call x0 -> x4, Pallas kernels: none -> 20.5 us  [accumulate(): pl.pallas_call(functools.partial(kernel, len(sources), prev is None, last...]
    ppermute x0 -> x9, starting transfers between devices: none -> 10.8 us  [swap(): return lax.ppermute(block, AXES, [(i, i ^ bit) for i in range(devices)])]
    ppermute x0 -> x9, waiting for transfers between devices: none -> 9.08 us  [swap(): return lax.ppermute(block, AXES, [(i, i ^ bit) for i in range(devices)])]
    select_n x16 -> x0, other arithmetic: 5.73 us -> none  [tensor_parts(): jnp.where(near, 1.0 - 9.0 / 32.0 * distance, 0.75 * inverse + 0.5 * cubed)]
    while x32 -> x0, local copies, waits for them, and re-layouts: 5.08 us -> none
    unnamed x0 -> x20, local copies, waits for them, and re-layouts: none -> 2.43 us
  transfers between devices with their start and end apart: 0 -> 9, of which waited for: 0 -> 6; matrix products, arithmetic and copies ran while one was open for 0% -> 0% of each run, Pallas kernels for 0% -> 34%
where the time goes in v1:
time: 44 us; the launch traced here: 43.6 us
  Pallas kernels  20.5 us (47%)
  starting transfers between devices  10.8 us (25%)
  waiting for transfers between devices  9.08 us (21%)
  local copies, waits for them, and re-layouts  2.51 us (6%)
  other arithmetic  0.78 us (2%)
    pallas_call x4, Pallas kernels, accumulate(): pl.pallas_call(functools.partial(kernel, len(sources), prev is None, last...  20.5 us
    ppermute x9, starting transfers between devices, swap(): return lax.ppermute(block, AXES, [(i, i ^ bit) for i in range(devices)])  10.8 us
    ppermute x9, waiting for transfers between devices, swap(): return lax.ppermute(block, AXES, [(i, i ^ bit) for i in range(devices)])  9.08 us
    unnamed x20, local copies, waits for them, and re-layouts  2.43 us
  transfers between devices with their start and end apart: 9, of which 6 were waited for; matrix products, arithmetic and copies ran while one was open for 0% of the time, Pallas kernels for 34%

profile of v1, /device:TPU:0, one launch (start us, length us, event | category | flops | bytes accessed | tf_op | source)
XLA Modules:
  0.0 43.6 jit_solution(13265961004750977089)
XLA Ops:
  0.0 0.1 pad.11.clone
  0.1 0.8 %maximum_maximum_fusion.tgt_ref = f32[8,256]{1,0:T(8,128)S(1)} fusion(f32[3,256]{1,0:T(4,128)} %param.3, f32[3,256]{1,0:T(4,128)} %param.2, f32[8]{0:T(128)S(1)} %pad.11.clone), kind=kLoop, calls=%fused_computation.3 | loop fusion | flops 4096 | bytes 14368 | tf_op jit(solution)/shard_map/concatenate | solution.py:102
  0.9 0.0 copy-start
  0.9 4.0 %collective-permute-start = (f32[1,8,256]{2,1,0:T(8,128)S(1)}, f32[1,8,256]{2,1,0:T(8,128)S(1)}, u32[]{:S(2)}, u32[]{:S(2)}) collective-permute-start(f32[1,8,256]{2,1,0:T(8,128)S(1)} %bitcast.1), channel_id=1, source_target_pairs={{0,16},{1,17},{2,18},{3,19},{4,20},{5,21},{6,22},{7,23},{8,24},{9,... | collective-permute-start | bytes 24584 | tf_op jit(solution)/shard_map/ppermute | solution.py:94
  4.9 1.6 %collective-permute-done.refs_1_ = f32[1,8,256]{2,1,0:T(8,128)S(1)} collective-permute-done((f32[1,8,256]{2,1,0:T(8,128)S(1)}, f32[1,8,256]{2,1,0:T(8,128)S(1)}, u32[]{:S(2)}, u32[]{:S(2)}) %collective-permute-start) | collective-permute-done | bytes 8224 | tf_op jit(solution)/shard_map/ppermute | solution.py:94
  6.5 0.0 copy-start.1
  6.5 1.9 %collective-permute-start.1 = (f32[2,8,256]{2,1,0:T(8,128)S(1)}, f32[2,8,256]{2,1,0:T(8,128)S(1)}, u32[]{:S(2)}, u32[]{:S(2)}) collective-permute-start(f32[2,8,256]{2,1,0:T(8,128)S(1)} %pad_maximum_fusion.2), channel_id=1, source_target_pairs={{0,8},{1,9},{2,10},{3,11},{4,12},{5,13},{6,14},{7,15},{8,0},{9,1},... | collective-permute-start | bytes 49160 | tf_op jit(solution)/shard_map/ppermute | solution.py:94
  8.4 1.8 %collective-permute-done.1.refs_2_ = f32[2,8,256]{2,1,0:T(8,128)S(1)} collective-permute-done((f32[2,8,256]{2,1,0:T(8,128)S(1)}, f32[2,8,256]{2,1,0:T(8,128)S(1)}, u32[]{:S(2)}, u32[]{:S(2)}) %collective-permute-start.1) | collective-permute-done | bytes 16416 | tf_op jit(solution)/shard_map/ppermute | solution.py:94
  10.3 0.0 copy-start.2
  10.3 1.8 %collective-permute-start.2 = (f32[4,8,256]{2,1,0:T(8,128)S(1)}, f32[4,8,256]{2,1,0:T(8,128)S(1)}, u32[]{:S(2)}, u32[]{:S(2)}) collective-permute-start(f32[4,8,256]{2,1,0:T(8,128)S(1)} %pad_maximum_fusion.1), channel_id=1, source_target_pairs={{0,4},{1,5},{2,6},{3,7},{4,0},{5,1},{6,2},{7,3},{8,12},{9,13},{10,... | collective-permute-start | bytes 98312 | tf_op jit(solution)/shard_map/ppermute | solution.py:94
  12.1 2.1 %collective-permute-done.2.refs_0_ = f32[4,8,256]{2,1,0:T(8,128)S(1)} collective-permute-done((f32[4,8,256]{2,1,0:T(8,128)S(1)}, f32[4,8,256]{2,1,0:T(8,128)S(1)}, u32[]{:S(2)}, u32[]{:S(2)}) %collective-permute-start.2) | collective-permute-done | bytes 32800 | tf_op jit(solution)/shard_map/ppermute | solution.py:94
  14.2 0.0 copy-start.3
  14.2 1.9 %collective-permute-start.3 = (f32[8,8,256]{2,1,0:T(8,128)S(1)}, f32[8,8,256]{2,1,0:T(8,128)S(1)}, u32[]{:S(2)}, u32[]{:S(2)}) collective-permute-start(f32[8,8,256]{2,1,0:T(8,128)S(1)} %pad_maximum_fusion), channel_id=1, source_target_pairs={{0,2},{1,3},{2,0},{3,1},{4,6},{5,7},{6,4},{7,5},{8,10},{9,11},{10,... | collective-permute-start | bytes 196616 | tf_op jit(solution)/shard_map/ppermute | solution.py:94
  16.1 2.4 %collective-permute-done.3.refs_0_ = f32[8,8,256]{2,1,0:T(8,128)S(1)} collective-permute-done((f32[8,8,256]{2,1,0:T(8,128)S(1)}, f32[8,8,256]{2,1,0:T(8,128)S(1)}, u32[]{:S(2)}, u32[]{:S(2)}) %collective-permute-start.3) | collective-permute-done | bytes 65568 | tf_op jit(solution)/shard_map/ppermute | solution.py:94
  18.5 0.0 copy-start.4
  18.5 0.0 collective-permute-start.4
  18.5 0.0 copy-done.3
  18.5 0.5 %collective-permute-start.5 = (f32[4,8,256]{2,1,0:T(8,128)S(1)}, f32[4,8,256]{2,1,0:T(8,128)S(1)}, u32[]{:S(2)}, u32[]{:S(2)}) collective-permute-start(f32[4,8,256]{2,1,0:T(8,128)S(1)} %collective-permute-done.2.refs_0_), channel_id=1, source_target_pairs={{0,1},{1,0},{2,3},{3,2},{4,5},{5,4},{6,7},{7,6},{8,9},{9,8},{10,11... | collective-permute-start | bytes 98312 | tf_op jit(solution)/shard_map/ppermute | solution.py:94
  19.1 0.0 copy-done.2
  19.1 0.1 collective-permute-start.8
  19.1 0.0 copy-done
  19.1 0.4 %collective-permute-start.6 = (f32[1,8,256]{2,1,0:T(8,128)S(1)}, f32[1,8,256]{2,1,0:T(8,128)S(1)}, u32[]{:S(2)}, u32[]{:S(2)}) collective-permute-start(f32[1,8,256]{2,1,0:T(8,128)S(1)} %bitcast.5), channel_id=1, source_target_pairs={{0,1},{1,0},{2,3},{3,2},{4,5},{5,4},{6,7},{7,6},{8,9},{9,8},{10,11... | collective-permute-start | bytes 24584 | tf_op jit(solution)/shard_map/ppermute | solution.py:94
  19.6 0.0 copy-done.1
  19.6 0.1 collective-permute-start.7
  19.6 0.8 %collective-permute-done.6.refs_3_ = f32[1,8,256]{2,1,0:T(8,128)S(1)} collective-permute-done((f32[1,8,256]{2,1,0:T(8,128)S(1)}, f32[1,8,256]{2,1,0:T(8,128)S(1)}, u32[]{:S(2)}, u32[]{:S(2)}) %collective-permute-start.6) | collective-permute-done | bytes 8224 | tf_op jit(solution)/shard_map/ppermute | solution.py:94
  20.4 0.0 copy-start.8
  20.4 0.3 collective-permute-done.7.refs_4_
  20.7 0.0 copy-start.9
  20.7 0.0 collective-permute-done.8.refs_5_
  20.7 0.2 copy-done.8
  21.0 0.3 copy-done.9
  21.3 0.0 copy-start.7
  21.3 0.6 %copy-done.7 = f32[2,8,256]{2,1,0:T(8,128)} copy-done((f32[2,8,256]{2,1,0:T(8,128)}, f32[2,8,256]{2,1,0:T(8,128)S(1)}, u32[]{:S(2)}) %copy-start.7) | copy-done | bytes 16408
  21.9 4.5 %shard_map.28.refs_2_ = f32[3,256,128]{2,1,0:T(8,128)} custom-call(f32[8,256]{1,0:T(8,128)} %copy-done, f32[1,8,256]{2,1,0:T(8,128)} %bitcast.6, f32[1,8,256]{2,1,0:T(8,128)} %copy-done.1, f32[2,8,256]{2,1,0:T(8,128)} %copy-done.2, f32[1,8,256]{2,1,0:T(8,128)} %copy-done.8, f32[1,8,256]{2,1,0:T(8,128)} %copy-done.9, f32[2,8,256]{2,1,0:T(8,128)} %copy-done.7), custom_call_target="tpu_custom_call" | custom-call | flops 19922944 | tf_op jit(solution)/shard_map/pallas_call | solution.py:80
  26.4 0.0 copy-done.4
  26.4 0.0 collective-permute-done.5.refs_1_
  26.4 0.0 copy-start.6
  26.4 0.6 %copy-done.6 = f32[4,8,256]{2,1,0:T(8,128)} copy-done((f32[4,8,256]{2,1,0:T(8,128)}, f32[4,8,256]{2,1,0:T(8,128)S(1)}, u32[]{:S(2)}) %copy-start.6) | copy-done | bytes 32792
  27.0 4.7 %shard_map.29.refs_1_ = f32[3,256,128]{2,1,0:T(8,128)} custom-call(f32[8,256]{1,0:T(8,128)} %copy-done, f32[4,8,256]{2,1,0:T(8,128)} %copy-done.3, f32[4,8,256]{2,1,0:T(8,128)} %copy-done.6, f32[3,256,128]{2,1,0:T(8,128)} %shard_map.28.refs_2_), custom_call_target="tpu_custom_call" | custom-call | flops 19922944 | tf_op jit(solution)/shard_map/pallas_call | solution.py:80
  31.8 5.5 %shard_map.30.refs_1_ = f32[3,256,128]{2,1,0:T(8,128)} custom-call(f32[8,256]{1,0:T(8,128)} %copy-done, f32[8,8,256]{2,1,0:T(8,128)} %copy-done.4, f32[3,256,128]{2,1,0:T(8,128)} %shard_map.29.refs_1_), custom_call_target="tpu_custom_call" | custom-call | flops 19922944 | tf_op jit(solution)/shard_map/pallas_call | solution.py:80
  37.3 0.0 collective-permute-done.4.refs_0_
  37.3 0.0 copy-start.5
  37.3 0.6 %copy-done.5 = f32[8,8,256]{2,1,0:T(8,128)} copy-done((f32[8,8,256]{2,1,0:T(8,128)}, f32[8,8,256]{2,1,0:T(8,128)S(1)}, u32[]{:S(2)}) %copy-start.5) | copy-done | bytes 65560
  37.9 5.8 %shard_map.31 = f32[3,256]{1,0:T(4,128)} custom-call(f32[8,256]{1,0:T(8,128)} %copy-done, f32[8,8,256]{2,1,0:T(8,128)} %copy-done.5, f32[3,256,128]{2,1,0:T(8,128)} %shard_map.30.refs_1_), custom_call_target="tpu_custom_call" | custom-call | flops 19922944 | tf_op jit(solution)/shard_map/pallas_call | solution.py:80
  (4 shorter events, 0.0 us)
Async XLA Ops:
  0.9 18.3 %copy-start = (f32[8,256]{1,0:T(8,128)}, f32[8,256]{1,0:T(8,128)S(1)}, u32[]{:S(2)}) copy-start(f32[8,256]{1,0:T(8,128)S(1)} %maximum_maximum_fusion.tgt_ref) | copy-start | bytes 24580
  0.9 5.7 %collective-permute-start = (f32[1,8,256]{2,1,0:T(8,128)S(1)}, f32[1,8,256]{2,1,0:T(8,128)S(1)}, u32[]{:S(2)}, u32[]{:S(2)}) collective-permute-start(f32[1,8,256]{2,1,0:T(8,128)S(1)} %bitcast.1), channel_id=1, source_target_pairs={{0,16},{1,17},{2,18},{3,19},{4,20},{5,21},{6,22},{7,23},{8,24},{9,... | collective-permute-start | bytes 24584 | tf_op jit(solution)/shard_map/ppermute | solution.py:94
  6.5 13.0 %copy-start.1 = (f32[1,8,256]{2,1,0:T(8,128)}, f32[1,8,256]{2,1,0:T(8,128)S(1)}, u32[]{:S(2)}) copy-start(f32[1,8,256]{2,1,0:T(8,128)S(1)} %collective-permute-done.refs_1_) | copy-start | bytes 24580
  6.5 3.7 %collective-permute-start.1 = (f32[2,8,256]{2,1,0:T(8,128)S(1)}, f32[2,8,256]{2,1,0:T(8,128)S(1)}, u32[]{:S(2)}, u32[]{:S(2)}) collective-permute-start(f32[2,8,256]{2,1,0:T(8,128)S(1)} %pad_maximum_fusion.2), channel_id=1, source_target_pairs={{0,8},{1,9},{2,10},{3,11},{4,12},{5,13},{6,14},{7,15},{8,0},{9,1},... | collective-permute-start | bytes 49160 | tf_op jit(solution)/shard_map/ppermute | solution.py:94
  10.3 8.8 %copy-start.2 = (f32[2,8,256]{2,1,0:T(8,128)}, f32[2,8,256]{2,1,0:T(8,128)S(1)}, u32[]{:S(2)}) copy-start(f32[2,8,256]{2,1,0:T(8,128)S(1)} %collective-permute-done.1.refs_2_) | copy-start | bytes 49156
  10.3 3.9 %collective-permute-start.2 = (f32[4,8,256]{2,1,0:T(8,128)S(1)}, f32[4,8,256]{2,1,0:T(8,128)S(1)}, u32[]{:S(2)}, u32[]{:S(2)}) collective-permute-start(f32[4,8,256]{2,1,0:T(8,128)S(1)} %pad_maximum_fusion.1), channel_id=1, source_target_pairs={{0,4},{1,5},{2,6},{3,7},{4,0},{5,1},{6,2},{7,3},{8,12},{9,13},{10,... | collective-permute-start | bytes 98312 | tf_op jit(solution)/shard_map/ppermute | solution.py:94
  14.2 4.3 %copy-start.3 = (f32[4,8,256]{2,1,0:T(8,128)}, f32[4,8,256]{2,1,0:T(8,128)S(1)}, u32[]{:S(2)}) copy-start(f32[4,8,256]{2,1,0:T(8,128)S(1)} %collective-permute-done.2.refs_0_) | copy-start | bytes 98308
  14.2 4.3 %collective-permute-start.3 = (f32[8,8,256]{2,1,0:T(8,128)S(1)}, f32[8,8,256]{2,1,0:T(8,128)S(1)}, u32[]{:S(2)}, u32[]{:S(2)}) collective-permute-start(f32[8,8,256]{2,1,0:T(8,128)S(1)} %pad_maximum_fusion), channel_id=1, source_target_pairs={{0,2},{1,3},{2,0},{3,1},{4,6},{5,7},{6,4},{7,5},{8,10},{9,11},{10,... | collective-permute-start | bytes 196616 | tf_op jit(solution)/shard_map/ppermute | solution.py:94
  18.5 7.9 %copy-start.4 = (f32[8,8,256]{2,1,0:T(8,128)}, f32[8,8,256]{2,1,0:T(8,128)S(1)}, u32[]{:S(2)}) copy-start(f32[8,8,256]{2,1,0:T(8,128)S(1)} %collective-permute-done.3.refs_0_) | copy-start | bytes 196612
  18.5 18.7 %collective-permute-start.4 = (f32[8,8,256]{2,1,0:T(8,128)S(1)}, f32[8,8,256]{2,1,0:T(8,128)S(1)}, u32[]{:S(2)}, u32[]{:S(2)}) collective-permute-start(f32[8,8,256]{2,1,0:T(8,128)S(1)} %collective-permute-done.3.refs_0_), channel_id=1, source_target_pairs={{0,1},{1,0},{2,3},{3,2},{4,5},{5,4},{6,7},{7,6},{8,9},{9,8},{10,11... | collective-permute-start | bytes 196616 | tf_op jit(solution)/shard_map/ppermute | solution.py:94
  18.5 7.9 %collective-permute-start.5 = (f32[4,8,256]{2,1,0:T(8,128)S(1)}, f32[4,8,256]{2,1,0:T(8,128)S(1)}, u32[]{:S(2)}, u32[]{:S(2)}) collective-permute-start(f32[4,8,256]{2,1,0:T(8,128)S(1)} %collective-permute-done.2.refs_0_), channel_id=1, source_target_pairs={{0,1},{1,0},{2,3},{3,2},{4,5},{5,4},{6,7},{7,6},{8,9},{9,8},{10,11... | collective-permute-start | bytes 98312 | tf_op jit(solution)/shard_map/ppermute | solution.py:94
  19.1 1.7 %collective-permute-start.8 = (f32[2,8,256]{2,1,0:T(8,128)S(1)}, f32[2,8,256]{2,1,0:T(8,128)S(1)}, u32[]{:S(2)}, u32[]{:S(2)}) collective-permute-start(f32[2,8,256]{2,1,0:T(8,128)S(1)} %collective-permute-done.1.refs_2_), channel_id=1, source_target_pairs={{0,1},{1,0},{2,3},{3,2},{4,5},{5,4},{6,7},{7,6},{8,9},{9,8},{10,11... | collective-permute-start | bytes 49160 | tf_op jit(solution)/shard_map/ppermute | solution.py:94
  19.1 1.3 %collective-permute-start.6 = (f32[1,8,256]{2,1,0:T(8,128)S(1)}, f32[1,8,256]{2,1,0:T(8,128)S(1)}, u32[]{:S(2)}, u32[]{:S(2)}) collective-permute-start(f32[1,8,256]{2,1,0:T(8,128)S(1)} %bitcast.5), channel_id=1, source_target_pairs={{0,1},{1,0},{2,3},{3,2},{4,5},{5,4},{6,7},{7,6},{8,9},{9,8},{10,11... | collective-permute-start | bytes 24584 | tf_op jit(solution)/shard_map/ppermute | solution.py:94
  19.6 1.2 %collective-permute-start.7 = (f32[1,8,256]{2,1,0:T(8,128)S(1)}, f32[1,8,256]{2,1,0:T(8,128)S(1)}, u32[]{:S(2)}, u32[]{:S(2)}) collective-permute-start(f32[1,8,256]{2,1,0:T(8,128)S(1)} %collective-permute-done.refs_1_), channel_id=1, source_target_pairs={{0,1},{1,0},{2,3},{3,2},{4,5},{5,4},{6,7},{7,6},{8,9},{9,8},{10,11... | collective-permute-start | bytes 24584 | tf_op jit(solution)/shard_map/ppermute | solution.py:94
  20.4 0.6 %copy-start.8 = (f32[1,8,256]{2,1,0:T(8,128)}, f32[1,8,256]{2,1,0:T(8,128)S(1)}, u32[]{:S(2)}) copy-start(f32[1,8,256]{2,1,0:T(8,128)S(1)} %collective-permute-done.6.refs_3_) | copy-start | bytes 24580
  20.7 0.6 %copy-start.9 = (f32[1,8,256]{2,1,0:T(8,128)}, f32[1,8,256]{2,1,0:T(8,128)S(1)}, u32[]{:S(2)}) copy-start(f32[1,8,256]{2,1,0:T(8,128)S(1)} %collective-permute-done.7.refs_4_) | copy-start | bytes 24580
  21.3 0.6 %copy-start.7 = (f32[2,8,256]{2,1,0:T(8,128)}, f32[2,8,256]{2,1,0:T(8,128)S(1)}, u32[]{:S(2)}) copy-start(f32[2,8,256]{2,1,0:T(8,128)S(1)} %collective-permute-done.8.refs_5_) | copy-start | bytes 49156
  26.4 0.6 %copy-start.6 = (f32[4,8,256]{2,1,0:T(8,128)}, f32[4,8,256]{2,1,0:T(8,128)S(1)}, u32[]{:S(2)}) copy-start(f32[4,8,256]{2,1,0:T(8,128)S(1)} %collective-permute-done.5.refs_1_) | copy-start | bytes 98308
  37.3 0.6 %copy-start.5 = (f32[8,8,256]{2,1,0:T(8,128)}, f32[8,8,256]{2,1,0:T(8,128)S(1)}, u32[]{:S(2)}) copy-start(f32[8,8,256]{2,1,0:T(8,128)S(1)} %collective-permute-done.4.refs_0_) | copy-start | bytes 196612

commit v2 on v1

--- a/solution.py
+++ b/solution.py
@@ -83,6 +83,7 @@
         in_specs=[VMEM] * len(args),
         out_specs=VMEM,
         scratch_shapes=[pltpu.VMEM(acc_shape, f32)] if last else [],
+        compiler_params=pltpu.CompilerParams(vmem_limit_bytes=8 * 1024 * 1024),
         cost_estimate=pl.CostEstimate(flops=38 * pairs, bytes_accessed=0, transcendentals=pairs),
     )(*args)
 
@@ -100,18 +101,27 @@
         bit //= 2
 
     own = jnp.concatenate([positions, forces, jnp.zeros((2, positions.shape[1]), f32)], axis=0)
-    target = own
-    held = own[None]
-    mine, theirs = [held], [swap(held, 1)]
-    for bit in bits:
+
+    held, fresh, acc = own[None], own[None], None
+    for step, bit in enumerate(bits):
+        late = step == len(bits) - 1
         got = swap(held, bit)
-        mine.append(got)
-        theirs.append(swap(got, 1))
-        held = jnp.concatenate([held, got], axis=0)
-    acc = accumulate(target, mine[:-2] + theirs[:-2], None, False)
-    acc = accumulate(target, [mine[-2], theirs[-2]], acc, False)
-    acc = accumulate(target, [mine[-1]], acc, False)
-    return accumulate(target, [theirs[-1]], acc, True)
+        if late:
+            across = swap(held, 1)
+            acc = accumulate(own, [fresh], acc, False)
+            across, acc = lax.optimization_barrier((across, acc))
+            acc = accumulate(own, [across], acc, False)
+        elif step > 0:
+            acc = accumulate(own, [fresh] if acc is not None else [held], acc, False)
+        if acc is not None:
+            got, acc = lax.optimization_barrier((got, acc))
+        fresh = got
+        if not late:
+            held = jnp.concatenate([held, got], axis=0)
+    across = swap(fresh, 1)
+    acc = accumulate(own, [fresh], acc, False)
+    across, acc = lax.optimization_barrier((across, acc))
+    return accumulate(own, [across], acc, True)
 
 
 def solution(mesh):

time: 44 us -> 30.2 us (0.69)
  waiting for transfers between devices: 9.08 us -> 3.8 us
  Pallas kernels: 20.5 us -> 15.4 us
  local copies, waits for them, and re-layouts: 2.51 us -> 0.08 us
  starting transfers between devices: 10.8 us -> 9.91 us
    ppermute x9 -> x6, waiting for transfers between devices: 9.08 us -> 3.8 us  [swap(): return lax.ppermute(block, AXES, [(i, i ^ bit) for i in range(devices)])]
    pallas_call x4 -> x6, Pallas kernels: 20.5 us -> 15.4 us  [accumulate(): pl.pallas_call(functools.partial(kernel, len(sources), prev is None, last...]
    unnamed x20 -> x0, local copies, waits for them, and re-layouts: 2.43 us -> none
    ppermute x9 -> x6, starting transfers between devices: 10.8 us -> 9.91 us  [swap(): return lax.ppermute(block, AXES, [(i, i ^ bit) for i in range(devices)])]
  transfers between devices with their start and end apart: 9 -> 6, of which waited for: 6 -> 3; matrix products, arithmetic and copies ran while one was open for 0% -> 0% of each run, Pallas kernels for 34% -> 36%
where the time goes in v2:
time: 30.2 us; the launch traced here: 30.1 us
  Pallas kernels  15.4 us (51%)
  starting transfers between devices  9.91 us (33%)
  waiting for transfers between devices  3.8 us (13%)
  other arithmetic  0.78 us (3%)
    pallas_call x6, Pallas kernels, accumulate(): pl.pallas_call(functools.partial(kernel, len(sources), prev is None, last...  15.4 us
    ppermute x6, starting transfers between devices, swap(): return lax.ppermute(block, AXES, [(i, i ^ bit) for i in range(devices)])  9.91 us
    ppermute x6, waiting for transfers between devices, swap(): return lax.ppermute(block, AXES, [(i, i ^ bit) for i in range(devices)])  3.8 us
    concatenate x1, other arithmetic, body(): jnp.concatenate([positions, forces, jnp.zeros((2, positions.shape[1]), f3...  0.77 us
  transfers between devices with their start and end apart: 6, of which 3 were waited for; matrix products, arithmetic and copies ran while one was open for 0% of the time, Pallas kernels for 36%

profile of v2, /device:TPU:0, one launch (start us, length us, event | category | flops | bytes accessed | tf_op | source)
XLA Modules:
  0.0 30.1 jit_solution(17529606551817999763)
XLA Ops:
  0.0 0.1 pad.11.clone
  0.1 0.8 %maximum_maximum_fusion.tgt_ref = f32[8,256]{1,0:T(8,128)S(1)} fusion(f32[3,256]{1,0:T(4,128)} %param.3, f32[3,256]{1,0:T(4,128)} %param.2, f32[8]{0:T(128)S(1)} %pad.11.clone), kind=kLoop, calls=%fused_computation.3 | loop fusion | flops 4096 | bytes 14368 | tf_op jit(solution)/shard_map/concatenate | solution.py:103
  0.9 4.0 %collective-permute-start = (f32[1,8,256]{2,1,0:T(8,128)S(1)}, f32[1,8,256]{2,1,0:T(8,128)S(1)}, u32[]{:S(2)}, u32[]{:S(2)}) collective-permute-start(f32[1,8,256]{2,1,0:T(8,128)S(1)} %bitcast.1), channel_id=1, source_target_pairs={{0,16},{1,17},{2,18},{3,19},{4,20},{5,21},{6,22},{7,23},{8,24},{9,... | collective-permute-start | bytes 24584 | tf_op jit(solution)/shard_map/ppermute | solution.py:95
  4.9 1.6 %collective-permute-done = f32[1,8,256]{2,1,0:T(8,128)S(1)} collective-permute-done((f32[1,8,256]{2,1,0:T(8,128)S(1)}, f32[1,8,256]{2,1,0:T(8,128)S(1)}, u32[]{:S(2)}, u32[]{:S(2)}) %collective-permute-start) | collective-permute-done | bytes 8224 | tf_op jit(solution)/shard_map/ppermute | solution.py:95
  6.5 1.9 %collective-permute-start.1 = (f32[2,8,256]{2,1,0:T(8,128)S(1)}, f32[2,8,256]{2,1,0:T(8,128)S(1)}, u32[]{:S(2)}, u32[]{:S(2)}) collective-permute-start(f32[2,8,256]{2,1,0:T(8,128)S(1)} %pad_maximum_fusion.2.refs_0_), channel_id=1, source_target_pairs={{0,8},{1,9},{2,10},{3,11},{4,12},{5,13},{6,14},{7,15},{8,0},{9,1},... | collective-permute-start | bytes 49160 | tf_op jit(solution)/shard_map/ppermute | solution.py:95
  8.4 0.9 %shard_map.28.refs_1_ = f32[3,256,128]{2,1,0:T(8,128)S(1)} custom-call(f32[8,256]{1,0:T(8,128)S(1)} %maximum_maximum_fusion.tgt_ref, f32[2,8,256]{2,1,0:T(8,128)S(1)} %pad_maximum_fusion.2.refs_0_), custom_call_target="tpu_custom_call" | custom-call | flops 4980736 | tf_op jit(solution)/shard_map/pallas_call | solution.py:80
  9.3 1.0 %collective-permute-done.1.refs_0_ = f32[2,8,256]{2,1,0:T(8,128)S(1)} collective-permute-done((f32[2,8,256]{2,1,0:T(8,128)S(1)}, f32[2,8,256]{2,1,0:T(8,128)S(1)}, u32[]{:S(2)}, u32[]{:S(2)}) %collective-permute-start.1) | collective-permute-done | bytes 16416 | tf_op jit(solution)/shard_map/ppermute | solution.py:95
  10.3 1.8 %collective-permute-start.2 = (f32[4,8,256]{2,1,0:T(8,128)S(1)}, f32[4,8,256]{2,1,0:T(8,128)S(1)}, u32[]{:S(2)}, u32[]{:S(2)}) collective-permute-start(f32[4,8,256]{2,1,0:T(8,128)S(1)} %pad_maximum_fusion.1), channel_id=1, source_target_pairs={{0,4},{1,5},{2,6},{3,7},{4,0},{5,1},{6,2},{7,3},{8,12},{9,13},{10,... | collective-permute-start | bytes 98312 | tf_op jit(solution)/shard_map/ppermute | solution.py:95
  12.1 0.9 %shard_map.29.refs_1_ = f32[3,256,128]{2,1,0:T(8,128)S(1)} custom-call(f32[8,256]{1,0:T(8,128)S(1)} %maximum_maximum_fusion.tgt_ref, f32[2,8,256]{2,1,0:T(8,128)S(1)} %collective-permute-done.1.refs_0_, f32[3,256,128]{2,1,0:T(8,128)S(1)} %shard_map.28.refs_1_), custom_call_target="tpu_custom_call" | custom-call | flops 4980736 | tf_op jit(solution)/shard_map/pallas_call | solution.py:80
  13.0 1.2 %collective-permute-done.2.refs_0_ = f32[4,8,256]{2,1,0:T(8,128)S(1)} collective-permute-done((f32[4,8,256]{2,1,0:T(8,128)S(1)}, f32[4,8,256]{2,1,0:T(8,128)S(1)}, u32[]{:S(2)}, u32[]{:S(2)}) %collective-permute-start.2) | collective-permute-done | bytes 32800 | tf_op jit(solution)/shard_map/ppermute | solution.py:95
  14.2 0.0 collective-permute-start.4
  14.2 1.9 %collective-permute-start.3 = (f32[8,8,256]{2,1,0:T(8,128)S(1)}, f32[8,8,256]{2,1,0:T(8,128)S(1)}, u32[]{:S(2)}, u32[]{:S(2)}) collective-permute-start(f32[8,8,256]{2,1,0:T(8,128)S(1)} %pad_maximum_fusion), channel_id=1, source_target_pairs={{0,2},{1,3},{2,0},{3,1},{4,6},{5,7},{6,4},{7,5},{8,10},{9,11},{10,... | collective-permute-start | bytes 196616 | tf_op jit(solution)/shard_map/ppermute | solution.py:95
  16.1 1.7 %shard_map.30.refs_1_ = f32[3,256,128]{2,1,0:T(8,128)S(1)} custom-call(f32[8,256]{1,0:T(8,128)S(1)} %maximum_maximum_fusion.tgt_ref, f32[4,8,256]{2,1,0:T(8,128)S(1)} %collective-permute-done.2.refs_0_, f32[3,256,128]{2,1,0:T(8,128)S(1)} %shard_map.29.refs_1_), custom_call_target="tpu_custom_call" | custom-call | flops 9961472 | tf_op jit(solution)/shard_map/pallas_call | solution.py:80
  17.8 0.0 collective-permute-done.4.refs_0_
  17.8 3.6 %shard_map.31.refs_1_ = f32[3,256,128]{2,1,0:T(8,128)S(1)} custom-call(f32[8,256]{1,0:T(8,128)S(1)} %maximum_maximum_fusion.tgt_ref, f32[8,8,256]{2,1,0:T(8,128)S(1)} %collective-permute-done.4.refs_0_, f32[3,256,128]{2,1,0:T(8,128)S(1)} %shard_map.30.refs_1_), custom_call_target="tpu_custom_call" | custom-call | flops 19922944 | tf_op jit(solution)/shard_map/pallas_call | solution.py:80
  21.4 0.0 collective-permute-done.3.refs_0_
  21.4 0.2 collective-permute-start.5
  21.7 3.7 %shard_map.32.refs_1_ = f32[3,256,128]{2,1,0:T(8,128)S(1)} custom-call(f32[8,256]{1,0:T(8,128)S(1)} %maximum_maximum_fusion.tgt_ref, f32[8,8,256]{2,1,0:T(8,128)S(1)} %collective-permute-done.3.refs_0_, f32[3,256,128]{2,1,0:T(8,128)S(1)} %shard_map.31.refs_1_), custom_call_target="tpu_custom_call" | custom-call | flops 19922944 | tf_op jit(solution)/shard_map/pallas_call | solution.py:80
  25.4 0.0 collective-permute-done.5.refs_0_
  25.4 4.7 %shard_map.33 = f32[3,256]{1,0:T(4,128)} custom-call(f32[8,256]{1,0:T(8,128)S(1)} %maximum_maximum_fusion.tgt_ref, f32[8,8,256]{2,1,0:T(8,128)S(1)} %collective-permute-done.5.refs_0_, f32[3,256,128]{2,1,0:T(8,128)S(1)} %shard_map.32.refs_1_), custom_call_target="tpu_custom_call" | custom-call | flops 19922944 | tf_op jit(solution)/shard_map/pallas_call | solution.py:80
  (4 shorter events, 0.0 us)
Async XLA Ops:
  0.9 5.7 %collective-permute-start = (f32[1,8,256]{2,1,0:T(8,128)S(1)}, f32[1,8,256]{2,1,0:T(8,128)S(1)}, u32[]{:S(2)}, u32[]{:S(2)}) collective-permute-start(f32[1,8,256]{2,1,0:T(8,128)S(1)} %bitcast.1), channel_id=1, source_target_pairs={{0,16},{1,17},{2,18},{3,19},{4,20},{5,21},{6,22},{7,23},{8,24},{9,... | collective-permute-start | bytes 24584 | tf_op jit(solution)/shard_map/ppermute | solution.py:95
  6.5 3.7 %collective-permute-start.1 = (f32[2,8,256]{2,1,0:T(8,128)S(1)}, f32[2,8,256]{2,1,0:T(8,128)S(1)}, u32[]{:S(2)}, u32[]{:S(2)}) collective-permute-start(f32[2,8,256]{2,1,0:T(8,128)S(1)} %pad_maximum_fusion.2.refs_0_), channel_id=1, source_target_pairs={{0,8},{1,9},{2,10},{3,11},{4,12},{5,13},{6,14},{7,15},{8,0},{9,1},... | collective-permute-start | bytes 49160 | tf_op jit(solution)/shard_map/ppermute | solution.py:95
  10.3 3.9 %collective-permute-start.2 = (f32[4,8,256]{2,1,0:T(8,128)S(1)}, f32[4,8,256]{2,1,0:T(8,128)S(1)}, u32[]{:S(2)}, u32[]{:S(2)}) collective-permute-start(f32[4,8,256]{2,1,0:T(8,128)S(1)} %pad_maximum_fusion.1), channel_id=1, source_target_pairs={{0,4},{1,5},{2,6},{3,7},{4,0},{5,1},{6,2},{7,3},{8,12},{9,13},{10,... | collective-permute-start | bytes 98312 | tf_op jit(solution)/shard_map/ppermute | solution.py:95
  14.2 3.6 %collective-permute-start.4 = (f32[8,8,256]{2,1,0:T(8,128)S(1)}, f32[8,8,256]{2,1,0:T(8,128)S(1)}, u32[]{:S(2)}, u32[]{:S(2)}) collective-permute-start(f32[8,8,256]{2,1,0:T(8,128)S(1)} %pad_maximum_fusion), channel_id=1, source_target_pairs={{0,1},{1,0},{2,3},{3,2},{4,5},{5,4},{6,7},{7,6},{8,9},{9,8},{10,11... | collective-permute-start | bytes 196616 | tf_op jit(solution)/shard_map/ppermute | solution.py:95
  14.2 7.2 %collective-permute-start.3 = (f32[8,8,256]{2,1,0:T(8,128)S(1)}, f32[8,8,256]{2,1,0:T(8,128)S(1)}, u32[]{:S(2)}, u32[]{:S(2)}) collective-permute-start(f32[8,8,256]{2,1,0:T(8,128)S(1)} %pad_maximum_fusion), channel_id=1, source_target_pairs={{0,2},{1,3},{2,0},{3,1},{4,6},{5,7},{6,4},{7,5},{8,10},{9,11},{10,... | collective-permute-start | bytes 196616 | tf_op jit(solution)/shard_map/ppermute | solution.py:95
  21.4 3.9 %collective-permute-start.5 = (f32[8,8,256]{2,1,0:T(8,128)S(1)}, f32[8,8,256]{2,1,0:T(8,128)S(1)}, u32[]{:S(2)}, u32[]{:S(2)}) collective-permute-start(f32[8,8,256]{2,1,0:T(8,128)S(1)} %collective-permute-done.3.refs_0_), channel_id=1, source_target_pairs={{0,1},{1,0},{2,3},{3,2},{4,5},{5,4},{6,7},{7,6},{8,9},{9,8},{10,11... | collective-permute-start | bytes 196616 | tf_op jit(solution)/shard_map/ppermute | solution.py:95

commit v3 on v1

v3 whole, which is shorter than its diff:
```python
import functools

import jax
import jax.numpy as jnp
from jax import lax
from jax.experimental import pallas as pl
from jax.experimental.pallas import tpu as pltpu
from jax.sharding import PartitionSpec as P

f32, bf16 = jnp.float32, jnp.bfloat16
AXES = ("row", "col")
LANES = 128
GROUP = 32
SUMS = 32
CONTRACT_LAST = (((1,), (1,)), ((), ()))
VMEM = pl.BlockSpec(memory_space=pltpu.VMEM)


def pieces(value):
    high = value.astype(bf16).astype(f32)
    rest = value - high
    middle = rest.astype(bf16).astype(f32)
    return high, middle, rest - middle


def halves(value):
    high = value.astype(bf16)
    return high, (value - high.astype(f32)).astype(bf16)


def prepare(tgt_ref, spread_ref, projector_ref):
    target = tgt_ref[...]
    count = target.shape[1]
    columns = jnp.transpose(target)
    for k in range(3):
        spread_ref[k] = jnp.broadcast_to(columns[:, k : k + 1], (count, LANES))
    none = jnp.zeros((3, count), f32)
    high, middle, low = pieces(
        jnp.concatenate(
            [none, 3.0 * target[0:3], jnp.full((1, count), -3.0, f32), none[0:1]], axis=0
        )
    )
    sides = jnp.concatenate([high, high, high, middle, middle, low], axis=0)
    projector_ref[...] = jnp.transpose(sides).astype(bf16)


def add_block(block, row, spread_ref, projector_ref, force_rows, total):
    targets, width = projector_ref.shape[0], row.shape[1]
    along = row[0:3] * row[3:6]
    along = along[0:1] + along[1:2] + along[2:3]
    high, middle, low = pieces(jnp.concatenate([row[0:6], along, row[7:8]], axis=0))
    sides = jnp.concatenate([high, middle, low, high, middle, high], axis=0)
    projection = jnp.dot(projector_ref[...], sides.astype(bf16), preferred_element_type=f32)
    columns = sides[0:SUMS]
    for_scalar = jnp.where(force_rows, columns, 0.0).astype(bf16)
    for_dyad = jnp.where(force_rows, 0.0, columns).astype(bf16)

    parts = [[], [], [], []]
    for base in range(0, targets, GROUP):
        offset = []
        for k in range(3):
            target = spread_ref[k, base : base + GROUP, :]
            target = jnp.concatenate([target] * (width // LANES), axis=1)
            offset.append(target - jnp.broadcast_to(block(k), (GROUP, width)))
        dx, dy, dz = offset
        squared = dx * dx + dy * dy + dz * dz
        along = jnp.where(squared <= 0.0, 0.0, projection[base : base + GROUP])
        inverse = lax.rsqrt(jnp.maximum(squared, 1e-12))
        capped = jnp.minimum(inverse, 0.5)
        q = capped * capped
        mixed = inverse * capped
        scalar = capped * (4.0 - (squared * mixed) * (2.5 - q))
        w = ((mixed * capped) * (0.5 - q)) * along
        for part, value in zip(parts, halves(scalar) + halves(w)):
            part.append(value)
    left = jnp.concatenate([jnp.concatenate(part, axis=0) for part in parts], axis=1)
    right = jnp.concatenate([for_scalar, for_scalar, for_dyad, for_dyad], axis=1)
    half = targets // 2
    return [
        now
        + lax.dot_general(
            left[at : at + half], right, CONTRACT_LAST, preferred_element_type=f32
        )
        for now, at in zip(total, (0, half))
    ]


def kernel(count, first, last, *refs):
    refs = list(refs)
    tgt_ref = refs.pop(0) if first or last else None
    spread_ref, projector_ref = (None, None) if first else (refs.pop(0), refs.pop(0))
    sources = [refs.pop(0) for _ in range(count)]
    prev_ref = None if first else refs.pop(0)
    if first:
        spread_ref, projector_ref = refs.pop(0), refs.pop(0)
        prepare(tgt_ref, spread_ref, projector_ref)
    out_ref = refs.pop(0)
    targets, width = projector_ref.shape[0], sources[0].shape[2]
    half = targets // 2

    index = lax.broadcasted_iota(jnp.int32, (SUMS, width), 0) & 7
    force_rows = (index >= 3) & (index < 6)
    if first:
        total = [jnp.zeros((half, SUMS), f32)] * 2
    else:
        total = [prev_ref[0:half], prev_ref[half:targets]]
    for ref in sources:
        blocks = ref.shape[0]
        together = min(blocks, 8)

        def step(i, total, ref=ref, together=together):
            for j in range(together):
                at = i * together + j
                total = add_block(
                    lambda k: ref[at, k : k + 1, :],
                    ref[at],
                    spread_ref,
                    projector_ref,
                    force_rows,
                    total,
                )
            return total

        if blocks == together:
            total = step(0, total)
        else:
            total = lax.fori_loop(0, blocks // together, step, total)
    if not last:
        out_ref[0:half] = total[0]
        out_ref[half:targets] = total[1]
        return
    wide = jnp.zeros((targets, LANES - SUMS), f32)
    sums = jnp.transpose(jnp.concatenate([jnp.concatenate(total, axis=0), wide], axis=1))
    sums = sums[0:8] + sums[8:16] + sums[16:24]
    out_ref[...] = 0.125 * (sums[3:6] + tgt_ref[0:3] * sums[7:8] - sums[0:3])


def accumulate(target, state, sources, last=False):
    targets = target.shape[1]
    first = state is None
    pairs = targets * sum(s.shape[0] * s.shape[2] for s in sources)
    total = jax.ShapeDtypeStruct((targets, SUMS), f32)
    args = ([target] if first or last else []) + (
        list(sources) if first else [*state[:2], *sources, state[2]]
    )
    if first:
        out = [
            jax.ShapeDtypeStruct((3, targets, LANES), f32),
            jax.ShapeDtypeStruct((targets, 48), bf16),
            total,
        ]
    else:
        out = jax.ShapeDtypeStruct((3, targets), f32) if last else total
    got = pl.pallas_call(
        functools.partial(kernel, len(sources), first, last),
        out_shape=out,
        in_specs=[VMEM] * len(args),
        out_specs=[VMEM] * 3 if first else VMEM,
        compiler_params=pltpu.CompilerParams(vmem_limit_bytes=16 * 1024 * 1024),
        cost_estimate=pl.CostEstimate(flops=38 * pairs, bytes_accessed=0, transcendentals=pairs),
    )(*args)
    if first:
        return tuple(got)
    return got if last else (*state[:2], got)


def body(sizes, positions, forces):
    devices = sizes[0] * sizes[1]

    def swap(block, bit):
        return lax.ppermute(block, AXES, [(i, i ^ bit) for i in range(devices)])

    def after(block, state):
        block, total = lax.optimization_barrier((block, state[2]))
        return block, (*state[:2], total)

    bits = []
    bit = devices // 2
    while bit > 1:
        bits.append(bit)
        bit //= 2

    block = jnp.concatenate([positions, forces, jnp.ones((2, positions.shape[1]), f32)], axis=0)[None]
    own = block[0]
    held, fresh, across, state = block, block, [], None
    for step, bit in enumerate(bits):
        got = swap(held, bit)
        state = accumulate(own, state, [fresh])
        if across:
            across[-1], state = after(across[-1], state)
            state = accumulate(own, state, across)
        got, state = after(got, state)
        across = [swap(got, 1)] if step else [swap(block, 1), swap(got, 1)]
        fresh = got
        if bit != bits[-1]:
            held = jnp.concatenate([held, got], axis=0)
    state = accumulate(own, state, [fresh])
    across[-1], state = after(across[-1], state)
    return accumulate(own, state, across, last=True)


def solution(mesh):
    sizes = (mesh.shape["row"], mesh.shape["col"])
    return jax.shard_map(
        functools.partial(body, sizes),
        mesh=mesh,
        in_specs=(P(None, AXES), P(None, AXES)),
        out_specs=P(None, AXES),
        check_vma=False,
    )
```

time: 44 us -> 24.7 us (0.56)
  Pallas kernels: 20.5 us -> 11.1 us
  waiting for transfers between devices: 9.08 us -> 2.47 us
  local copies, waits for them, and re-layouts: 2.51 us -> 0.08 us
  starting transfers between devices: 10.8 us -> 10 us
    pallas_call x4 -> x9, Pallas kernels: 20.5 us -> 11.1 us  [accumulate(): pl.pallas_call(functools.partial(kernel, len(sources), first, last), out_...]
    ppermute x9, waiting for transfers between devices: 9.08 us -> 2.47 us  [swap(): return lax.ppermute(block, AXES, [(i, i ^ bit) for i in range(devices)])]
    unnamed x20 -> x0, local copies, waits for them, and re-layouts: 2.43 us -> none
    ppermute x9, starting transfers between devices: 10.8 us -> 10 us  [swap(): return lax.ppermute(block, AXES, [(i, i ^ bit) for i in range(devices)])]
  transfers between devices with their start and end apart: 9 -> 9, of which waited for: 6 -> 6; matrix products, arithmetic and copies ran while one was open for 0% -> 0% of each run, Pallas kernels for 34% -> 33%
where the time goes in v3:
time: 24.7 us; the launch traced here: 24.6 us
  Pallas kernels  11.1 us (45%)
  starting transfers between devices  10 us (40%)
  waiting for transfers between devices  2.47 us (10%)
  other arithmetic  0.79 us (3%)
    pallas_call x9, Pallas kernels, accumulate(): pl.pallas_call(functools.partial(kernel, len(sources), first, last), out_...  11.1 us
    ppermute x9, starting transfers between devices, swap(): return lax.ppermute(block, AXES, [(i, i ^ bit) for i in range(devices)])  10 us
    ppermute x9, waiting for transfers between devices, swap(): return lax.ppermute(block, AXES, [(i, i ^ bit) for i in range(devices)])  2.47 us
    concatenate x1, other arithmetic, body(): jnp.concatenate([positions, forces, jnp.ones((2, positions.shape[1]), f32...  0.77 us
  transfers between devices with their start and end apart: 9, of which 6 were waited for; matrix products, arithmetic and copies ran while one was open for 0% of the time, Pallas kernels for 33%

profile of v3, /device:TPU:0, one launch (start us, length us, event | category | flops | bytes accessed | tf_op | source)
XLA Modules:
  0.0 24.6 jit_solution(15851233953435888998)
XLA Ops:
  0.0 0.1 pad.11.clone
  0.1 0.8 %maximum_maximum_fusion.refs_0_ = f32[8,256]{1,0:T(8,128)S(1)} fusion(f32[3,256]{1,0:T(4,128)} %param.3, f32[3,256]{1,0:T(4,128)} %param.2, f32[8]{0:T(128)S(1)} %pad.11.clone), kind=kLoop, calls=%fused_computation.3 | loop fusion | flops 4096 | bytes 14368 | tf_op jit(solution)/shard_map/concatenate | solution.py:183
  0.9 4.0 %collective-permute-start = (f32[1,8,256]{2,1,0:T(8,128)S(1)}, f32[1,8,256]{2,1,0:T(8,128)S(1)}, u32[]{:S(2)}, u32[]{:S(2)}) collective-permute-start(f32[1,8,256]{2,1,0:T(8,128)S(1)} %bitcast.1), channel_id=1, source_target_pairs={{0,16},{1,17},{2,18},{3,19},{4,20},{5,21},{6,22},{7,23},{8,24},{9,... | collective-permute-start | bytes 24584 | tf_op jit(solution)/shard_map/ppermute | solution.py:171
  4.9 0.7 %shard_map.28 = (f32[3,256,128]{2,1,0:T(8,128)S(1)}, bf16[256,48]{1,0:T(8,128)(2,1)S(1)}, f32[256,32]{1,0:T(8,128)S(1)}) custom-call(f32[8,256]{1,0:T(8,128)S(1)} %maximum_maximum_fusion.refs_0_, f32[1,8,256]{2,1,0:T(8,128)S(1)} %bitcast.2), custom_call_target="tpu_custom_call" | custom-call | flops 2490368 | tf_op jit(solution)/shard_map/pallas_call | solution.py:154
  5.6 0.9 %collective-permute-done.refs_2_ = f32[1,8,256]{2,1,0:T(8,128)S(1)} collective-permute-done((f32[1,8,256]{2,1,0:T(8,128)S(1)}, f32[1,8,256]{2,1,0:T(8,128)S(1)}, u32[]{:S(2)}, u32[]{:S(2)}) %collective-permute-start) | collective-permute-done | bytes 8224 | tf_op jit(solution)/shard_map/ppermute | solution.py:171
  6.5 1.9 %collective-permute-start.1 = (f32[2,8,256]{2,1,0:T(8,128)S(1)}, f32[2,8,256]{2,1,0:T(8,128)S(1)}, u32[]{:S(2)}, u32[]{:S(2)}) collective-permute-start(f32[2,8,256]{2,1,0:T(8,128)S(1)} %pad_maximum_fusion.2), channel_id=1, source_target_pairs={{0,8},{1,9},{2,10},{3,11},{4,12},{5,13},{6,14},{7,15},{8,0},{9,1},... | collective-permute-start | bytes 49160 | tf_op jit(solution)/shard_map/ppermute | solution.py:171
  8.4 0.0 collective-permute-start.3
  8.4 0.5 %collective-permute-start.2 = (f32[1,8,256]{2,1,0:T(8,128)S(1)}, f32[1,8,256]{2,1,0:T(8,128)S(1)}, u32[]{:S(2)}, u32[]{:S(2)}) collective-permute-start(f32[1,8,256]{2,1,0:T(8,128)S(1)} %bitcast.4), channel_id=1, source_target_pairs={{0,1},{1,0},{2,3},{3,2},{4,5},{5,4},{6,7},{7,6},{8,9},{9,8},{10,11... | collective-permute-start | bytes 24584 | tf_op jit(solution)/shard_map/ppermute | solution.py:171
  8.9 0.4 %shard_map.29.refs_4_ = f32[256,32]{1,0:T(8,128)S(1)} custom-call(f32[3,256,128]{2,1,0:T(8,128)S(1)} %get-tuple-element.24.refs_0_.refs_1_, bf16[256,48]{1,0:T(8,128)(2,1)S(1)} %get-tuple-element.25.refs_1_.refs_2_, f32[1,8,256]{2,1,0:T(8,128)S(1)} %collective-permute-done.refs_2_, f32[256,32]{1,0:T(8,128)S(1)} %get-tuple-element.28.refs_3_), custom_call_target="tpu_custom_call" | custom-call | flops 2490368 | tf_op jit(solution)/shard_map/pallas_call | solution.py:154
  9.4 0.2 collective-permute-done.3.refs_3_
  9.6 0.2 collective-permute-done.2.refs_2_
  9.8 0.7 %shard_map.30.refs_3_ = f32[256,32]{1,0:T(8,128)S(1)} custom-call(f32[3,256,128]{2,1,0:T(8,128)S(1)} %get-tuple-element.24.refs_0_.refs_1_, bf16[256,48]{1,0:T(8,128)(2,1)S(1)} %get-tuple-element.25.refs_1_.refs_2_, f32[1,8,256]{2,1,0:T(8,128)S(1)} %collective-permute-done.2.refs_2_, f32[1,8,256]{2,1,0:T(8,128)S(1)} %collective-permute-done.3.refs_3_, ...), custom_call_target="tpu_custom_call" | custom-call | flops 4980736 | tf_op jit(solution)/shard_map/pallas_call | solution.py:154
  10.5 0.0 collective-permute-done.1.refs_2_
  10.5 1.6 %collective-permute-start.4 = (f32[4,8,256]{2,1,0:T(8,128)S(1)}, f32[4,8,256]{2,1,0:T(8,128)S(1)}, u32[]{:S(2)}, u32[]{:S(2)}) collective-permute-start(f32[4,8,256]{2,1,0:T(8,128)S(1)} %pad_maximum_fusion.1), channel_id=1, source_target_pairs={{0,4},{1,5},{2,6},{3,7},{4,0},{5,1},{6,2},{7,3},{8,12},{9,13},{10,... | collective-permute-start | bytes 98312 | tf_op jit(solution)/shard_map/ppermute | solution.py:171
  12.1 0.0 collective-permute-start.5
  12.1 0.7 %shard_map.31.refs_3_ = f32[256,32]{1,0:T(8,128)S(1)} custom-call(f32[3,256,128]{2,1,0:T(8,128)S(1)} %get-tuple-element.24.refs_0_.refs_1_, bf16[256,48]{1,0:T(8,128)(2,1)S(1)} %get-tuple-element.25.refs_1_.refs_2_, f32[2,8,256]{2,1,0:T(8,128)S(1)} %collective-permute-done.1.refs_2_, f32[256,32]{1,0:T(8,128)S(1)} %shard_map.30.refs_3_), custom_call_target="tpu_custom_call" | custom-call | flops 4980736 | tf_op jit(solution)/shard_map/pallas_call | solution.py:154
  12.8 0.4 %collective-permute-done.5.refs_2_ = f32[2,8,256]{2,1,0:T(8,128)S(1)} collective-permute-done((f32[2,8,256]{2,1,0:T(8,128)S(1)}, f32[2,8,256]{2,1,0:T(8,128)S(1)}, u32[]{:S(2)}, u32[]{:S(2)}) %collective-permute-start.5) | collective-permute-done | bytes 16416 | tf_op jit(solution)/shard_map/ppermute | solution.py:171
  13.3 0.7 %shard_map.32.refs_3_ = f32[256,32]{1,0:T(8,128)S(1)} custom-call(f32[3,256,128]{2,1,0:T(8,128)S(1)} %get-tuple-element.24.refs_0_.refs_1_, bf16[256,48]{1,0:T(8,128)(2,1)S(1)} %get-tuple-element.25.refs_1_.refs_2_, f32[2,8,256]{2,1,0:T(8,128)S(1)} %collective-permute-done.5.refs_2_, f32[256,32]{1,0:T(8,128)S(1)} %shard_map.31.refs_3_), custom_call_target="tpu_custom_call" | custom-call | flops 4980736 | tf_op jit(solution)/shard_map/pallas_call | solution.py:154
  14.0 0.5 %collective-permute-done.4.refs_2_ = f32[4,8,256]{2,1,0:T(8,128)S(1)} collective-permute-done((f32[4,8,256]{2,1,0:T(8,128)S(1)}, f32[4,8,256]{2,1,0:T(8,128)S(1)}, u32[]{:S(2)}, u32[]{:S(2)}) %collective-permute-start.4) | collective-permute-done | bytes 32800 | tf_op jit(solution)/shard_map/ppermute | solution.py:171
  14.5 1.5 %collective-permute-start.6 = (f32[8,8,256]{2,1,0:T(8,128)S(1)}, f32[8,8,256]{2,1,0:T(8,128)S(1)}, u32[]{:S(2)}, u32[]{:S(2)}) collective-permute-start(f32[8,8,256]{2,1,0:T(8,128)S(1)} %pad_maximum_fusion), channel_id=1, source_target_pairs={{0,2},{1,3},{2,0},{3,1},{4,6},{5,7},{6,4},{7,5},{8,10},{9,11},{10,... | collective-permute-start | bytes 196616 | tf_op jit(solution)/shard_map/ppermute | solution.py:171
  16.0 0.0 collective-permute-start.7
  16.0 1.3 %shard_map.33.refs_3_ = f32[256,32]{1,0:T(8,128)S(1)} custom-call(f32[3,256,128]{2,1,0:T(8,128)S(1)} %get-tuple-element.24.refs_0_.refs_1_, bf16[256,48]{1,0:T(8,128)(2,1)S(1)} %get-tuple-element.25.refs_1_.refs_2_, f32[4,8,256]{2,1,0:T(8,128)S(1)} %collective-permute-done.4.refs_2_, f32[256,32]{1,0:T(8,128)S(1)} %shard_map.32.refs_3_), custom_call_target="tpu_custom_call" | custom-call | flops 9961472 | tf_op jit(solution)/shard_map/pallas_call | solution.py:154
  17.3 0.0 collective-permute-done.7.refs_2_
  17.3 1.3 %shard_map.34.refs_3_ = f32[256,32]{1,0:T(8,128)S(1)} custom-call(f32[3,256,128]{2,1,0:T(8,128)S(1)} %get-tuple-element.24.refs_0_.refs_1_, bf16[256,48]{1,0:T(8,128)(2,1)S(1)} %get-tuple-element.25.refs_1_.refs_2_, f32[4,8,256]{2,1,0:T(8,128)S(1)} %collective-permute-done.7.refs_2_, f32[256,32]{1,0:T(8,128)S(1)} %shard_map.33.refs_3_), custom_call_target="tpu_custom_call" | custom-call | flops 9961472 | tf_op jit(solution)/shard_map/pallas_call | solution.py:154
  18.6 0.2 collective-permute-done.6.refs_2_
  18.8 0.4 %collective-permute-start.8 = (f32[8,8,256]{2,1,0:T(8,128)S(1)}, f32[8,8,256]{2,1,0:T(8,128)S(1)}, u32[]{:S(2)}, u32[]{:S(2)}) collective-permute-start(f32[8,8,256]{2,1,0:T(8,128)S(1)} %collective-permute-done.6.refs_2_), channel_id=1, source_target_pairs={{0,1},{1,0},{2,3},{3,2},{4,5},{5,4},{6,7},{7,6},{8,9},{9,8},{10,11... | collective-permute-start | bytes 196616 | tf_op jit(solution)/shard_map/ppermute | solution.py:171
  19.2 2.4 %shard_map.35.refs_4_ = f32[256,32]{1,0:T(8,128)S(1)} custom-call(f32[3,256,128]{2,1,0:T(8,128)S(1)} %get-tuple-element.24.refs_0_.refs_1_, bf16[256,48]{1,0:T(8,128)(2,1)S(1)} %get-tuple-element.25.refs_1_.refs_2_, f32[8,8,256]{2,1,0:T(8,128)S(1)} %collective-permute-done.6.refs_2_, f32[256,32]{1,0:T(8,128)S(1)} %shard_map.34.refs_3_), custom_call_target="tpu_custom_call" | custom-call | flops 19922944 | tf_op jit(solution)/shard_map/pallas_call | solution.py:154
  21.5 0.0 collective-permute-done.8.refs_3_
  21.5 3.0 %shard_map.36 = f32[3,256]{1,0:T(4,128)} custom-call(f32[8,256]{1,0:T(8,128)S(1)} %maximum_maximum_fusion.refs_0_, f32[3,256,128]{2,1,0:T(8,128)S(1)} %get-tuple-element.24.refs_0_.refs_1_, bf16[256,48]{1,0:T(8,128)(2,1)S(1)} %get-tuple-element.25.refs_1_.refs_2_, f32[8,8,256]{2,1,0:T(8,128)S(1)} %collective-permute-done.8.refs_3_, ...), custom_call_target="tpu_custom_call" | custom-call | flops 19922944 | tf_op jit(solution)/shard_map/pallas_call | solution.py:154
  (4 shorter events, 0.0 us)
Async XLA Ops:
  0.9 5.7 %collective-permute-start = (f32[1,8,256]{2,1,0:T(8,128)S(1)}, f32[1,8,256]{2,1,0:T(8,128)S(1)}, u32[]{:S(2)}, u32[]{:S(2)}) collective-permute-start(f32[1,8,256]{2,1,0:T(8,128)S(1)} %bitcast.1), channel_id=1, source_target_pairs={{0,16},{1,17},{2,18},{3,19},{4,20},{5,21},{6,22},{7,23},{8,24},{9,... | collective-permute-start | bytes 24584 | tf_op jit(solution)/shard_map/ppermute | solution.py:171
  6.5 4.0 %collective-permute-start.1 = (f32[2,8,256]{2,1,0:T(8,128)S(1)}, f32[2,8,256]{2,1,0:T(8,128)S(1)}, u32[]{:S(2)}, u32[]{:S(2)}) collective-permute-start(f32[2,8,256]{2,1,0:T(8,128)S(1)} %pad_maximum_fusion.2), channel_id=1, source_target_pairs={{0,8},{1,9},{2,10},{3,11},{4,12},{5,13},{6,14},{7,15},{8,0},{9,1},... | collective-permute-start | bytes 49160 | tf_op jit(solution)/shard_map/ppermute | solution.py:171
  8.4 1.2 %collective-permute-start.3 = (f32[1,8,256]{2,1,0:T(8,128)S(1)}, f32[1,8,256]{2,1,0:T(8,128)S(1)}, u32[]{:S(2)}, u32[]{:S(2)}) collective-permute-start(f32[1,8,256]{2,1,0:T(8,128)S(1)} %collective-permute-done.refs_2_), channel_id=1, source_target_pairs={{0,1},{1,0},{2,3},{3,2},{4,5},{5,4},{6,7},{7,6},{8,9},{9,8},{10,11... | collective-permute-start | bytes 24584 | tf_op jit(solution)/shard_map/ppermute | solution.py:171
  8.4 1.3 %collective-permute-start.2 = (f32[1,8,256]{2,1,0:T(8,128)S(1)}, f32[1,8,256]{2,1,0:T(8,128)S(1)}, u32[]{:S(2)}, u32[]{:S(2)}) collective-permute-start(f32[1,8,256]{2,1,0:T(8,128)S(1)} %bitcast.4), channel_id=1, source_target_pairs={{0,1},{1,0},{2,3},{3,2},{4,5},{5,4},{6,7},{7,6},{8,9},{9,8},{10,11... | collective-permute-start | bytes 24584 | tf_op jit(solution)/shard_map/ppermute | solution.py:171
  10.5 4.0 %collective-permute-start.4 = (f32[4,8,256]{2,1,0:T(8,128)S(1)}, f32[4,8,256]{2,1,0:T(8,128)S(1)}, u32[]{:S(2)}, u32[]{:S(2)}) collective-permute-start(f32[4,8,256]{2,1,0:T(8,128)S(1)} %pad_maximum_fusion.1), channel_id=1, source_target_pairs={{0,4},{1,5},{2,6},{3,7},{4,0},{5,1},{6,2},{7,3},{8,12},{9,13},{10,... | collective-permute-start | bytes 98312 | tf_op jit(solution)/shard_map/ppermute | solution.py:171
  12.1 1.2 %collective-permute-start.5 = (f32[2,8,256]{2,1,0:T(8,128)S(1)}, f32[2,8,256]{2,1,0:T(8,128)S(1)}, u32[]{:S(2)}, u32[]{:S(2)}) collective-permute-start(f32[2,8,256]{2,1,0:T(8,128)S(1)} %collective-permute-done.1.refs_2_), channel_id=1, source_target_pairs={{0,1},{1,0},{2,3},{3,2},{4,5},{5,4},{6,7},{7,6},{8,9},{9,8},{10,11... | collective-permute-start | bytes 49160 | tf_op jit(solution)/shard_map/ppermute | solution.py:171
  14.5 4.3 %collective-permute-start.6 = (f32[8,8,256]{2,1,0:T(8,128)S(1)}, f32[8,8,256]{2,1,0:T(8,128)S(1)}, u32[]{:S(2)}, u32[]{:S(2)}) collective-permute-start(f32[8,8,256]{2,1,0:T(8,128)S(1)} %pad_maximum_fusion), channel_id=1, source_target_pairs={{0,2},{1,3},{2,0},{3,1},{4,6},{5,7},{6,4},{7,5},{8,10},{9,11},{10,... | collective-permute-start | bytes 196616 | tf_op jit(solution)/shard_map/ppermute | solution.py:171
  16.0 1.3 %collective-permute-start.7 = (f32[4,8,256]{2,1,0:T(8,128)S(1)}, f32[4,8,256]{2,1,0:T(8,128)S(1)}, u32[]{:S(2)}, u32[]{:S(2)}) collective-permute-start(f32[4,8,256]{2,1,0:T(8,128)S(1)} %collective-permute-done.4.refs_2_), channel_id=1, source_target_pairs={{0,1},{1,0},{2,3},{3,2},{4,5},{5,4},{6,7},{7,6},{8,9},{9,8},{10,11... | collective-permute-start | bytes 98312 | tf_op jit(solution)/shard_map/ppermute | solution.py:171
  18.8 2.8 %collective-permute-start.8 = (f32[8,8,256]{2,1,0:T(8,128)S(1)}, f32[8,8,256]{2,1,0:T(8,128)S(1)}, u32[]{:S(2)}, u32[]{:S(2)}) collective-permute-start(f32[8,8,256]{2,1,0:T(8,128)S(1)} %collective-permute-done.6.refs_2_), channel_id=1, source_target_pairs={{0,1},{1,0},{2,3},{3,2},{4,5},{5,4},{6,7},{7,6},{8,9},{9,8},{10,11... | collective-permute-start | bytes 196616 | tf_op jit(solution)/shard_map/ppermute | solution.py:171

commit v4 on v3

--- a/solution.py
+++ b/solution.py
@@ -31,7 +31,7 @@
 def prepare(tgt_ref, spread_ref, projector_ref):
     target = tgt_ref[...]
     count = target.shape[1]
-    columns = jnp.transpose(target)
+    columns = jnp.transpose(jnp.concatenate([target, target[0:2]], axis=0))
     for k in range(3):
         spread_ref[k] = jnp.broadcast_to(columns[:, k : k + 1], (count, LANES))
     none = jnp.zeros((3, count), f32)
@@ -48,7 +48,7 @@
     targets, width = projector_ref.shape[0], row.shape[1]
     along = row[0:3] * row[3:6]
     along = along[0:1] + along[1:2] + along[2:3]
-    high, middle, low = pieces(jnp.concatenate([row[0:6], along, row[7:8]], axis=0))
+    high, middle, low = pieces(jnp.concatenate([row, along, jnp.ones_like(along)], axis=0))
     sides = jnp.concatenate([high, middle, low, high, middle, high], axis=0)
     projection = jnp.dot(projector_ref[...], sides.astype(bf16), preferred_element_type=f32)
     columns = sides[0:SUMS]
@@ -65,12 +65,12 @@
         dx, dy, dz = offset
         squared = dx * dx + dy * dy + dz * dz
         along = jnp.where(squared <= 0.0, 0.0, projection[base : base + GROUP])
-        inverse = lax.rsqrt(jnp.maximum(squared, 1e-12))
-        capped = jnp.minimum(inverse, 0.5)
+        inverse = lax.rsqrt(jnp.maximum(squared, 2.25e-12))
+        capped = jnp.minimum(inverse, 1.0 / 3.0)
         q = capped * capped
         mixed = inverse * capped
-        scalar = capped * (4.0 - (squared * mixed) * (2.5 - q))
-        w = ((mixed * capped) * (0.5 - q)) * along
+        scalar = capped * ((q + 5.0 / 3.0) - squared * mixed)
+        w = ((mixed * capped) * (2.0 / 9.0 - q)) * along
         for part, value in zip(parts, halves(scalar) + halves(w)):
             part.append(value)
     left = jnp.concatenate([jnp.concatenate(part, axis=0) for part in parts], axis=1)
@@ -132,7 +132,7 @@
     wide = jnp.zeros((targets, LANES - SUMS), f32)
     sums = jnp.transpose(jnp.concatenate([jnp.concatenate(total, axis=0), wide], axis=1))
     sums = sums[0:8] + sums[8:16] + sums[16:24]
-    out_ref[...] = 0.125 * (sums[3:6] + tgt_ref[0:3] * sums[7:8] - sums[0:3])
+    out_ref[...] = 0.421875 * (sums[3:6] + tgt_ref[0:3] * sums[7:8] - sums[0:3])
 
 
 def accumulate(target, state, sources, last=False):
@@ -180,23 +180,27 @@
         bits.append(bit)
         bit //= 2
 
-    block = jnp.concatenate([positions, forces, jnp.ones((2, positions.shape[1]), f32)], axis=0)[None]
+    block = jnp.concatenate([1.5 * positions, forces], axis=0)[None]
     own = block[0]
-    held, fresh, across, state = block, block, [], None
+    held, fresh, state = block, block, None
     for step, bit in enumerate(bits):
-        got = swap(held, bit)
+        got = swap(held, bit | 1)
+        known = len(bits) - step - 1
+        if known == 1:
+            across = swap(held, 1)
         state = accumulate(own, state, [fresh])
-        if across:
-            across[-1], state = after(across[-1], state)
-            state = accumulate(own, state, across)
+        if known < 2:
+            across, state = after(across, state)
+            state = accumulate(own, state, [across])
         got, state = after(got, state)
-        across = [swap(got, 1)] if step else [swap(block, 1), swap(got, 1)]
+        if known < 2:
+            across = swap(got, 1)
         fresh = got
-        if bit != bits[-1]:
+        if known:
             held = jnp.concatenate([held, got], axis=0)
     state = accumulate(own, state, [fresh])
-    across[-1], state = after(across[-1], state)
-    return accumulate(own, state, across, last=True)
+    across, state = after(across, state)
+    return accumulate(own, state, [across], last=True)
 
 
 def solution(mesh):

time: 24.7 us -> 22.9 us (0.927)
  waiting for transfers between devices: 2.47 us -> 1.7 us
  starting transfers between devices: 10 us -> 9.52 us
  Pallas kernels: 11.1 us -> 10.7 us
    concatenate x1 -> x0, other arithmetic: 0.77 us -> none  [body(): jnp.concatenate([positions, forces, jnp.ones((2, positions.shape[1]), f32...]
    ppermute x9 -> x7, waiting for transfers between devices: 2.47 us -> 1.7 us  [swap(): return lax.ppermute(block, AXES, [(i, i ^ bit) for i in range(devices)])]
    mul x0 -> x1, other arithmetic: none -> 0.7 us  [body(): block = jnp.concatenate([1.5 * positions, forces], axis=0)[None]]
    ppermute x9 -> x7, starting transfers between devices: 10 us -> 9.52 us  [swap(): return lax.ppermute(block, AXES, [(i, i ^ bit) for i in range(devices)])]
    pallas_call x9 -> x8, Pallas kernels: 11.1 us -> 10.7 us  [accumulate(): pl.pallas_call(functools.partial(kernel, len(sources), first, last), out_...]
  transfers between devices with their start and end apart: 9 -> 7, of which waited for: 6 -> 2; matrix products, arithmetic and copies ran while one was open for 0% -> 0% of each run, Pallas kernels for 33% -> 34%
where the time goes in v4:
time: 22.9 us; the launch traced here: 22.8 us
  Pallas kernels  10.7 us (47%)
  starting transfers between devices  9.52 us (42%)
  waiting for transfers between devices  1.7 us (7%)
  other arithmetic  0.73 us (3%)
    pallas_call x8, Pallas kernels, accumulate(): pl.pallas_call(functools.partial(kernel, len(sources), first, last), out_...  10.7 us
    ppermute x7, starting transfers between devices, swap(): return lax.ppermute(block, AXES, [(i, i ^ bit) for i in range(devices)])  9.52 us
    ppermute x7, waiting for transfers between devices, swap(): return lax.ppermute(block, AXES, [(i, i ^ bit) for i in range(devices)])  1.7 us
    mul x1, other arithmetic, body(): block = jnp.concatenate([1.5 * positions, forces], axis=0)[None]  0.7 us
  transfers between devices with their start and end apart: 7, of which 2 were waited for; matrix products, arithmetic and copies ran while one was open for 0% of the time, Pallas kernels for 34%

profile of v4, /device:TPU:0, one launch (start us, length us, event | category | flops | bytes accessed | tf_op | source)
XLA Modules:
  0.0 22.8 jit_solution(418300272855348618)
XLA Ops:
  0.0 0.0 copy-start
  0.0 0.7 %broadcast_multiply_fusion = f32[3,256]{1,0:T(4,128)S(1)} fusion(f32[3,256]{1,0:T(4,128)} %param.2), kind=kLoop, calls=%fused_computation.4 | loop fusion | flops 768 | bytes 6144 | tf_op jit(solution)/shard_map/mul | solution.py:183
  0.7 0.0 copy-done
  0.7 3.5 %collective-permute-start = (f32[1,6,256]{2,1,0:T(8,128)S(1)}, f32[1,6,256]{2,1,0:T(8,128)S(1)}, u32[]{:S(2)}, u32[]{:S(2)}) collective-permute-start(f32[1,6,256]{2,1,0:T(8,128)S(1)} %get-tuple-element.39.refs_1_), channel_id=1, source_target_pairs={{0,17},{1,16},{2,19},{3,18},{4,21},{5,20},{6,23},{7,22},{8,25},{9,... | collective-permute-start | bytes 18440 | tf_op jit(solution)/shard_map/ppermute | solution.py:171
  4.3 0.7 %shard_map.28 = (f32[3,256,128]{2,1,0:T(8,128)S(1)}, bf16[256,48]{1,0:T(8,128)(2,1)S(1)}, f32[256,32]{1,0:T(8,128)S(1)}) custom-call(f32[6,256]{1,0:T(8,128)S(1)} %get-tuple-element.40.refs_0_, f32[1,6,256]{2,1,0:T(8,128)S(1)} %get-tuple-element.39.refs_1_), custom_call_target="tpu_custom_call" | custom-call | flops 2490368 | tf_op jit(solution)/shard_map/pallas_call | solution.py:154
  4.9 0.7 %collective-permute-done.refs_2_ = f32[1,6,256]{2,1,0:T(8,128)S(1)} collective-permute-done((f32[1,6,256]{2,1,0:T(8,128)S(1)}, f32[1,6,256]{2,1,0:T(8,128)S(1)}, u32[]{:S(2)}, u32[]{:S(2)}) %collective-permute-start) | collective-permute-done | bytes 6176 | tf_op jit(solution)/shard_map/ppermute | solution.py:171
  5.6 1.9 %collective-permute-start.1 = (f32[2,6,256]{2,1,0:T(8,128)S(1)}, f32[2,6,256]{2,1,0:T(8,128)S(1)}, u32[]{:S(2)}, u32[]{:S(2)}) collective-permute-start(f32[2,6,256]{2,1,0:T(8,128)S(1)} %pad_maximum_fusion.2), channel_id=1, source_target_pairs={{0,9},{1,8},{2,11},{3,10},{4,13},{5,12},{6,15},{7,14},{8,1},{9,0},... | collective-permute-start | bytes 36872 | tf_op jit(solution)/shard_map/ppermute | solution.py:171
  7.5 0.4 %shard_map.29.refs_3_ = f32[256,32]{1,0:T(8,128)S(1)} custom-call(f32[3,256,128]{2,1,0:T(8,128)S(1)} %get-tuple-element.22.refs_0_.refs_1_, bf16[256,48]{1,0:T(8,128)(2,1)S(1)} %get-tuple-element.23.refs_1_.refs_2_, f32[1,6,256]{2,1,0:T(8,128)S(1)} %collective-permute-done.refs_2_, f32[256,32]{1,0:T(8,128)S(1)} %get-tuple-element.26.refs_3_), custom_call_target="tpu_custom_call" | custom-call | flops 2490368 | tf_op jit(solution)/shard_map/pallas_call | solution.py:154
  7.9 1.0 %collective-permute-done.1.refs_2_ = f32[2,6,256]{2,1,0:T(8,128)S(1)} collective-permute-done((f32[2,6,256]{2,1,0:T(8,128)S(1)}, f32[2,6,256]{2,1,0:T(8,128)S(1)}, u32[]{:S(2)}, u32[]{:S(2)}) %collective-permute-start.1) | collective-permute-done | bytes 12320 | tf_op jit(solution)/shard_map/ppermute | solution.py:171
  9.0 0.5 %collective-permute-start.3 = (f32[4,6,256]{2,1,0:T(8,128)S(1)}, f32[4,6,256]{2,1,0:T(8,128)S(1)}, u32[]{:S(2)}, u32[]{:S(2)}) collective-permute-start(f32[4,6,256]{2,1,0:T(8,128)S(1)} %pad_maximum_fusion.1), channel_id=1, source_target_pairs={{0,1},{1,0},{2,3},{3,2},{4,5},{5,4},{6,7},{7,6},{8,9},{9,8},{10,11... | collective-permute-start | bytes 73736 | tf_op jit(solution)/shard_map/ppermute | solution.py:171
  9.4 1.5 %collective-permute-start.2 = (f32[4,6,256]{2,1,0:T(8,128)S(1)}, f32[4,6,256]{2,1,0:T(8,128)S(1)}, u32[]{:S(2)}, u32[]{:S(2)}) collective-permute-start(f32[4,6,256]{2,1,0:T(8,128)S(1)} %pad_maximum_fusion.1), channel_id=1, source_target_pairs={{0,5},{1,4},{2,7},{3,6},{4,1},{5,0},{6,3},{7,2},{8,13},{9,12},{10,... | collective-permute-start | bytes 73736 | tf_op jit(solution)/shard_map/ppermute | solution.py:171
  11.0 0.7 %shard_map.30.refs_3_ = f32[256,32]{1,0:T(8,128)S(1)} custom-call(f32[3,256,128]{2,1,0:T(8,128)S(1)} %get-tuple-element.22.refs_0_.refs_1_, bf16[256,48]{1,0:T(8,128)(2,1)S(1)} %get-tuple-element.23.refs_1_.refs_2_, f32[2,6,256]{2,1,0:T(8,128)S(1)} %collective-permute-done.1.refs_2_, f32[256,32]{1,0:T(8,128)S(1)} %shard_map.29.refs_3_), custom_call_target="tpu_custom_call" | custom-call | flops 4980736 | tf_op jit(solution)/shard_map/pallas_call | solution.py:154
  11.7 0.0 collective-permute-done.3.refs_2_
  11.7 1.2 %shard_map.31.refs_3_ = f32[256,32]{1,0:T(8,128)S(1)} custom-call(f32[3,256,128]{2,1,0:T(8,128)S(1)} %get-tuple-element.22.refs_0_.refs_1_, bf16[256,48]{1,0:T(8,128)(2,1)S(1)} %get-tuple-element.23.refs_1_.refs_2_, f32[4,6,256]{2,1,0:T(8,128)S(1)} %collective-permute-done.3.refs_2_, f32[256,32]{1,0:T(8,128)S(1)} %shard_map.30.refs_3_), custom_call_target="tpu_custom_call" | custom-call | flops 9961472 | tf_op jit(solution)/shard_map/pallas_call | solution.py:154
  12.9 0.0 collective-permute-done.2.refs_2_
  12.9 1.5 %collective-permute-start.4 = (f32[8,6,256]{2,1,0:T(8,128)S(1)}, f32[8,6,256]{2,1,0:T(8,128)S(1)}, u32[]{:S(2)}, u32[]{:S(2)}) collective-permute-start(f32[8,6,256]{2,1,0:T(8,128)S(1)} %pad_maximum_fusion), channel_id=1, source_target_pairs={{0,3},{1,2},{2,1},{3,0},{4,7},{5,6},{6,5},{7,4},{8,11},{9,10},{10,... | collective-permute-start | bytes 147464 | tf_op jit(solution)/shard_map/ppermute | solution.py:171
  14.4 0.2 collective-permute-start.5
  14.6 1.2 %shard_map.32.refs_3_ = f32[256,32]{1,0:T(8,128)S(1)} custom-call(f32[3,256,128]{2,1,0:T(8,128)S(1)} %get-tuple-element.22.refs_0_.refs_1_, bf16[256,48]{1,0:T(8,128)(2,1)S(1)} %get-tuple-element.23.refs_1_.refs_2_, f32[4,6,256]{2,1,0:T(8,128)S(1)} %collective-permute-done.2.refs_2_, f32[256,32]{1,0:T(8,128)S(1)} %shard_map.31.refs_3_), custom_call_target="tpu_custom_call" | custom-call | flops 9961472 | tf_op jit(solution)/shard_map/pallas_call | solution.py:154
  15.9 0.0 collective-permute-done.5.refs_2_
  15.9 1.2 %shard_map.33.refs_3_ = f32[256,32]{1,0:T(8,128)S(1)} custom-call(f32[3,256,128]{2,1,0:T(8,128)S(1)} %get-tuple-element.22.refs_0_.refs_1_, bf16[256,48]{1,0:T(8,128)(2,1)S(1)} %get-tuple-element.23.refs_1_.refs_2_, f32[4,6,256]{2,1,0:T(8,128)S(1)} %collective-permute-done.5.refs_2_, f32[256,32]{1,0:T(8,128)S(1)} %shard_map.32.refs_3_), custom_call_target="tpu_custom_call" | custom-call | flops 9961472 | tf_op jit(solution)/shard_map/pallas_call | solution.py:154
  17.1 0.0 collective-permute-done.4.refs_2_
  17.1 0.4 %collective-permute-start.6 = (f32[8,6,256]{2,1,0:T(8,128)S(1)}, f32[8,6,256]{2,1,0:T(8,128)S(1)}, u32[]{:S(2)}, u32[]{:S(2)}) collective-permute-start(f32[8,6,256]{2,1,0:T(8,128)S(1)} %collective-permute-done.4.refs_2_), channel_id=1, source_target_pairs={{0,1},{1,0},{2,3},{3,2},{4,5},{5,4},{6,7},{7,6},{8,9},{9,8},{10,11... | collective-permute-start | bytes 147464 | tf_op jit(solution)/shard_map/ppermute | solution.py:171
  17.5 2.3 %shard_map.34.refs_4_ = f32[256,32]{1,0:T(8,128)S(1)} custom-call(f32[3,256,128]{2,1,0:T(8,128)S(1)} %get-tuple-element.22.refs_0_.refs_1_, bf16[256,48]{1,0:T(8,128)(2,1)S(1)} %get-tuple-element.23.refs_1_.refs_2_, f32[8,6,256]{2,1,0:T(8,128)S(1)} %collective-permute-done.4.refs_2_, f32[256,32]{1,0:T(8,128)S(1)} %shard_map.33.refs_3_), custom_call_target="tpu_custom_call" | custom-call | flops 19922944 | tf_op jit(solution)/shard_map/pallas_call | solution.py:154
  19.8 0.0 collective-permute-done.6.refs_3_
  19.8 3.0 %shard_map.35 = f32[3,256]{1,0:T(4,128)} custom-call(f32[6,256]{1,0:T(8,128)S(1)} %get-tuple-element.40.refs_0_, f32[3,256,128]{2,1,0:T(8,128)S(1)} %get-tuple-element.22.refs_0_.refs_1_, bf16[256,48]{1,0:T(8,128)(2,1)S(1)} %get-tuple-element.23.refs_1_.refs_2_, f32[8,6,256]{2,1,0:T(8,128)S(1)} %collective-permute-done.6.refs_3_, ...), custom_call_target="tpu_custom_call" | custom-call | flops 19922944 | tf_op jit(solution)/shard_map/pallas_call | solution.py:154
  (4 shorter events, 0.0 us)
Async XLA Ops:
  0.0 0.7 %copy-start = (f32[3,256]{1,0:T(4,128)S(1)}, f32[3,256]{1,0:T(4,128)}, u32[]{:S(2)}) copy-start(f32[3,256]{1,0:T(4,128)} %param.3) | copy-start | bytes 9220
  0.7 4.9 %collective-permute-start = (f32[1,6,256]{2,1,0:T(8,128)S(1)}, f32[1,6,256]{2,1,0:T(8,128)S(1)}, u32[]{:S(2)}, u32[]{:S(2)}) collective-permute-start(f32[1,6,256]{2,1,0:T(8,128)S(1)} %get-tuple-element.39.refs_1_), channel_id=1, source_target_pairs={{0,17},{1,16},{2,19},{3,18},{4,21},{5,20},{6,23},{7,22},{8,25},{9,... | collective-permute-start | bytes 18440 | tf_op jit(solution)/shard_map/ppermute | solution.py:171
  5.6 3.3 %collective-permute-start.1 = (f32[2,6,256]{2,1,0:T(8,128)S(1)}, f32[2,6,256]{2,1,0:T(8,128)S(1)}, u32[]{:S(2)}, u32[]{:S(2)}) collective-permute-start(f32[2,6,256]{2,1,0:T(8,128)S(1)} %pad_maximum_fusion.2), channel_id=1, source_target_pairs={{0,9},{1,8},{2,11},{3,10},{4,13},{5,12},{6,15},{7,14},{8,1},{9,0},... | collective-permute-start | bytes 36872 | tf_op jit(solution)/shard_map/ppermute | solution.py:171
  9.0 2.7 %collective-permute-start.3 = (f32[4,6,256]{2,1,0:T(8,128)S(1)}, f32[4,6,256]{2,1,0:T(8,128)S(1)}, u32[]{:S(2)}, u32[]{:S(2)}) collective-permute-start(f32[4,6,256]{2,1,0:T(8,128)S(1)} %pad_maximum_fusion.1), channel_id=1, source_target_pairs={{0,1},{1,0},{2,3},{3,2},{4,5},{5,4},{6,7},{7,6},{8,9},{9,8},{10,11... | collective-permute-start | bytes 73736 | tf_op jit(solution)/shard_map/ppermute | solution.py:171
  9.4 3.5 %collective-permute-start.2 = (f32[4,6,256]{2,1,0:T(8,128)S(1)}, f32[4,6,256]{2,1,0:T(8,128)S(1)}, u32[]{:S(2)}, u32[]{:S(2)}) collective-permute-start(f32[4,6,256]{2,1,0:T(8,128)S(1)} %pad_maximum_fusion.1), channel_id=1, source_target_pairs={{0,5},{1,4},{2,7},{3,6},{4,1},{5,0},{6,3},{7,2},{8,13},{9,12},{10,... | collective-permute-start | bytes 73736 | tf_op jit(solution)/shard_map/ppermute | solution.py:171
  12.9 4.2 %collective-permute-start.4 = (f32[8,6,256]{2,1,0:T(8,128)S(1)}, f32[8,6,256]{2,1,0:T(8,128)S(1)}, u32[]{:S(2)}, u32[]{:S(2)}) collective-permute-start(f32[8,6,256]{2,1,0:T(8,128)S(1)} %pad_maximum_fusion), channel_id=1, source_target_pairs={{0,3},{1,2},{2,1},{3,0},{4,7},{5,6},{6,5},{7,4},{8,11},{9,10},{10,... | collective-permute-start | bytes 147464 | tf_op jit(solution)/shard_map/ppermute | solution.py:171
  14.4 1.4 %collective-permute-start.5 = (f32[4,6,256]{2,1,0:T(8,128)S(1)}, f32[4,6,256]{2,1,0:T(8,128)S(1)}, u32[]{:S(2)}, u32[]{:S(2)}) collective-permute-start(f32[4,6,256]{2,1,0:T(8,128)S(1)} %collective-permute-done.2.refs_2_), channel_id=1, source_target_pairs={{0,1},{1,0},{2,3},{3,2},{4,5},{5,4},{6,7},{7,6},{8,9},{9,8},{10,11... | collective-permute-start | bytes 73736 | tf_op jit(solution)/shard_map/ppermute | solution.py:171
  17.1 2.7 %collective-permute-start.6 = (f32[8,6,256]{2,1,0:T(8,128)S(1)}, f32[8,6,256]{2,1,0:T(8,128)S(1)}, u32[]{:S(2)}, u32[]{:S(2)}) collective-permute-start(f32[8,6,256]{2,1,0:T(8,128)S(1)} %collective-permute-done.4.refs_2_), channel_id=1, source_target_pairs={{0,1},{1,0},{2,3},{3,2},{4,5},{5,4},{6,7},{7,6},{8,9},{9,8},{10,11... | collective-permute-start | bytes 147464 | tf_op jit(solution)/shard_map/ppermute | solution.py:171

commit v5 on v4

--- a/solution.py
+++ b/solution.py
@@ -44,7 +44,7 @@
     projector_ref[...] = jnp.transpose(sides).astype(bf16)
 
 
-def add_block(block, row, spread_ref, projector_ref, force_rows, total):
+def add_block(block, row, spread_ref, projector_ref, total):
     targets, width = projector_ref.shape[0], row.shape[1]
     along = row[0:3] * row[3:6]
     along = along[0:1] + along[1:2] + along[2:3]
@@ -52,8 +52,8 @@
     sides = jnp.concatenate([high, middle, low, high, middle, high], axis=0)
     projection = jnp.dot(projector_ref[...], sides.astype(bf16), preferred_element_type=f32)
     columns = sides[0:SUMS]
-    for_scalar = jnp.where(force_rows, columns, 0.0).astype(bf16)
-    for_dyad = jnp.where(force_rows, 0.0, columns).astype(bf16)
+    side = columns.astype(bf16)
+    side = jnp.concatenate([side, side], axis=1)
 
     parts = [[], [], [], []]
     for base in range(0, targets, GROUP):
@@ -73,16 +73,20 @@
         w = ((mixed * capped) * (2.0 / 9.0 - q)) * along
         for part, value in zip(parts, halves(scalar) + halves(w)):
             part.append(value)
-    left = jnp.concatenate([jnp.concatenate(part, axis=0) for part in parts], axis=1)
-    right = jnp.concatenate([for_scalar, for_scalar, for_dyad, for_dyad], axis=1)
+    parts = [jnp.concatenate(part, axis=0) for part in parts]
     half = targets // 2
-    return [
-        now
-        + lax.dot_general(
-            left[at : at + half], right, CONTRACT_LAST, preferred_element_type=f32
+    sums = []
+    for now, (pair, at) in zip(total, [(p, at) for p in (parts[:2], parts[2:]) for at in (0, half)]):
+        sums.append(
+            now
+            + lax.dot_general(
+                jnp.concatenate([part[at : at + half] for part in pair], axis=1),
+                side,
+                CONTRACT_LAST,
+                preferred_element_type=f32,
+            )
         )
-        for now, at in zip(total, (0, half))
-    ]
+    return sums
 
 
 def kernel(count, first, last, *refs):
@@ -95,15 +99,13 @@
         spread_ref, projector_ref = refs.pop(0), refs.pop(0)
         prepare(tgt_ref, spread_ref, projector_ref)
     out_ref = refs.pop(0)
-    targets, width = projector_ref.shape[0], sources[0].shape[2]
+    targets = projector_ref.shape[0]
     half = targets // 2
 
-    index = lax.broadcasted_iota(jnp.int32, (SUMS, width), 0) & 7
-    force_rows = (index >= 3) & (index < 6)
-    if first:
-        total = [jnp.zeros((half, SUMS), f32)] * 2
+    if first:
+        total = [jnp.zeros((half, SUMS), f32)] * 4
     else:
-        total = [prev_ref[0:half], prev_ref[half:targets]]
+        total = [prev_ref[i * half : i * half + half] for i in range(4)]
     for ref in sources:
         blocks = ref.shape[0]
         together = min(blocks, 8)
@@ -116,7 +118,6 @@
                     ref[at],
                     spread_ref,
                     projector_ref,
-                    force_rows,
                     total,
                 )
             return total
@@ -126,11 +127,14 @@
         else:
             total = lax.fori_loop(0, blocks // together, step, total)
     if not last:
-        out_ref[0:half] = total[0]
-        out_ref[half:targets] = total[1]
+        for i in range(4):
+            out_ref[i * half : i * half + half] = total[i]
         return
     wide = jnp.zeros((targets, LANES - SUMS), f32)
-    sums = jnp.transpose(jnp.concatenate([jnp.concatenate(total, axis=0), wide], axis=1))
+    lane = lax.broadcasted_iota(jnp.int32, (targets, SUMS), 1) & 7
+    scalar_sums, dyad_sums = (jnp.concatenate(total[i : i + 2], axis=0) for i in (0, 2))
+    total = jnp.where((lane >= 3) & (lane < 6), scalar_sums, dyad_sums)
+    sums = jnp.transpose(jnp.concatenate([total, wide], axis=1))
     sums = sums[0:8] + sums[8:16] + sums[16:24]
     out_ref[...] = 0.421875 * (sums[3:6] + tgt_ref[0:3] * sums[7:8] - sums[0:3])
 
@@ -139,7 +143,7 @@
     targets = target.shape[1]
     first = state is None
     pairs = targets * sum(s.shape[0] * s.shape[2] for s in sources)
-    total = jax.ShapeDtypeStruct((targets, SUMS), f32)
+    total = jax.ShapeDtypeStruct((2 * targets, SUMS), f32)
     args = ([target] if first or last else []) + (
         list(sources) if first else [*state[:2], *sources, state[2]]
     )

time: 22.9 us -> 22.9 us (level)
  no operation moved by 1% of the time
where the time goes in v5:
time: 22.9 us; the launch traced here: 22.7 us
  Pallas kernels  10.6 us (46%)
  starting transfers between devices  9.53 us (42%)
  waiting for transfers between devices  1.72 us (8%)
  other arithmetic  0.73 us (3%)
    pallas_call x8, Pallas kernels, accumulate(): pl.pallas_call(functools.partial(kernel, len(sources), first, last), out_...  10.6 us
    ppermute x7, starting transfers between devices, swap(): return lax.ppermute(block, AXES, [(i, i ^ bit) for i in range(devices)])  9.53 us
    ppermute x7, waiting for transfers between devices, swap(): return lax.ppermute(block, AXES, [(i, i ^ bit) for i in range(devices)])  1.72 us
    mul x1, other arithmetic, body(): block = jnp.concatenate([1.5 * positions, forces], axis=0)[None]  0.7 us
  transfers between devices with their start and end apart: 7, of which 2 were waited for; matrix products, arithmetic and copies ran while one was open for 0% of the time, Pallas kernels for 34%

profile of v5, /device:TPU:0, one launch (start us, length us, event | category | flops | bytes accessed | tf_op | source)
XLA Modules:
  0.0 22.7 jit_solution(3835970157130016649)
XLA Ops:
  0.0 0.0 copy-start
  0.0 0.7 %broadcast_multiply_fusion = f32[3,256]{1,0:T(4,128)S(1)} fusion(f32[3,256]{1,0:T(4,128)} %param.2), kind=kLoop, calls=%fused_computation.4 | loop fusion | flops 768 | bytes 6144 | tf_op jit(solution)/shard_map/mul | solution.py:187
  0.7 0.0 copy-done
  0.7 3.5 %collective-permute-start = (f32[1,6,256]{2,1,0:T(8,128)S(1)}, f32[1,6,256]{2,1,0:T(8,128)S(1)}, u32[]{:S(2)}, u32[]{:S(2)}) collective-permute-start(f32[1,6,256]{2,1,0:T(8,128)S(1)} %get-tuple-element.39.refs_1_), channel_id=1, source_target_pairs={{0,17},{1,16},{2,19},{3,18},{4,21},{5,20},{6,23},{7,22},{8,25},{9,... | collective-permute-start | bytes 18440 | tf_op jit(solution)/shard_map/ppermute | solution.py:175
  4.3 0.7 %shard_map.28 = (f32[3,256,128]{2,1,0:T(8,128)S(1)}, bf16[256,48]{1,0:T(8,128)(2,1)S(1)}, f32[512,32]{1,0:T(8,128)S(1)}) custom-call(f32[6,256]{1,0:T(8,128)S(1)} %get-tuple-element.40.refs_0_, f32[1,6,256]{2,1,0:T(8,128)S(1)} %get-tuple-element.39.refs_1_), custom_call_target="tpu_custom_call" | custom-call | flops 2490368 | tf_op jit(solution)/shard_map/pallas_call | solution.py:158
  5.0 0.7 %collective-permute-done.refs_2_ = f32[1,6,256]{2,1,0:T(8,128)S(1)} collective-permute-done((f32[1,6,256]{2,1,0:T(8,128)S(1)}, f32[1,6,256]{2,1,0:T(8,128)S(1)}, u32[]{:S(2)}, u32[]{:S(2)}) %collective-permute-start) | collective-permute-done | bytes 6176 | tf_op jit(solution)/shard_map/ppermute | solution.py:175
  5.6 1.9 %collective-permute-start.1 = (f32[2,6,256]{2,1,0:T(8,128)S(1)}, f32[2,6,256]{2,1,0:T(8,128)S(1)}, u32[]{:S(2)}, u32[]{:S(2)}) collective-permute-start(f32[2,6,256]{2,1,0:T(8,128)S(1)} %pad_maximum_fusion.2), channel_id=1, source_target_pairs={{0,9},{1,8},{2,11},{3,10},{4,13},{5,12},{6,15},{7,14},{8,1},{9,0},... | collective-permute-start | bytes 36872 | tf_op jit(solution)/shard_map/ppermute | solution.py:175
  7.5 0.4 %shard_map.29.refs_3_ = f32[512,32]{1,0:T(8,128)S(1)} custom-call(f32[3,256,128]{2,1,0:T(8,128)S(1)} %get-tuple-element.22.refs_0_.refs_1_, bf16[256,48]{1,0:T(8,128)(2,1)S(1)} %get-tuple-element.23.refs_1_.refs_2_, f32[1,6,256]{2,1,0:T(8,128)S(1)} %collective-permute-done.refs_2_, f32[512,32]{1,0:T(8,128)S(1)} %get-tuple-element.26.refs_3_), custom_call_target="tpu_custom_call" | custom-call | flops 2490368 | tf_op jit(solution)/shard_map/pallas_call | solution.py:158
  7.9 1.0 %collective-permute-done.1.refs_2_ = f32[2,6,256]{2,1,0:T(8,128)S(1)} collective-permute-done((f32[2,6,256]{2,1,0:T(8,128)S(1)}, f32[2,6,256]{2,1,0:T(8,128)S(1)}, u32[]{:S(2)}, u32[]{:S(2)}) %collective-permute-start.1) | collective-permute-done | bytes 12320 | tf_op jit(solution)/shard_map/ppermute | solution.py:175
  9.0 0.5 %collective-permute-start.3 = (f32[4,6,256]{2,1,0:T(8,128)S(1)}, f32[4,6,256]{2,1,0:T(8,128)S(1)}, u32[]{:S(2)}, u32[]{:S(2)}) collective-permute-start(f32[4,6,256]{2,1,0:T(8,128)S(1)} %pad_maximum_fusion.1), channel_id=1, source_target_pairs={{0,1},{1,0},{2,3},{3,2},{4,5},{5,4},{6,7},{7,6},{8,9},{9,8},{10,11... | collective-permute-start | bytes 73736 | tf_op jit(solution)/shard_map/ppermute | solution.py:175
  9.4 1.5 %collective-permute-start.2 = (f32[4,6,256]{2,1,0:T(8,128)S(1)}, f32[4,6,256]{2,1,0:T(8,128)S(1)}, u32[]{:S(2)}, u32[]{:S(2)}) collective-permute-start(f32[4,6,256]{2,1,0:T(8,128)S(1)} %pad_maximum_fusion.1), channel_id=1, source_target_pairs={{0,5},{1,4},{2,7},{3,6},{4,1},{5,0},{6,3},{7,2},{8,13},{9,12},{10,... | collective-permute-start | bytes 73736 | tf_op jit(solution)/shard_map/ppermute | solution.py:175
  11.0 0.7 %shard_map.30.refs_3_ = f32[512,32]{1,0:T(8,128)S(1)} custom-call(f32[3,256,128]{2,1,0:T(8,128)S(1)} %get-tuple-element.22.refs_0_.refs_1_, bf16[256,48]{1,0:T(8,128)(2,1)S(1)} %get-tuple-element.23.refs_1_.refs_2_, f32[2,6,256]{2,1,0:T(8,128)S(1)} %collective-permute-done.1.refs_2_, f32[512,32]{1,0:T(8,128)S(1)} %shard_map.29.refs_3_), custom_call_target="tpu_custom_call" | custom-call | flops 4980736 | tf_op jit(solution)/shard_map/pallas_call | solution.py:158
  11.7 0.0 collective-permute-done.3.refs_2_
  11.7 1.2 %shard_map.31.refs_3_ = f32[512,32]{1,0:T(8,128)S(1)} custom-call(f32[3,256,128]{2,1,0:T(8,128)S(1)} %get-tuple-element.22.refs_0_.refs_1_, bf16[256,48]{1,0:T(8,128)(2,1)S(1)} %get-tuple-element.23.refs_1_.refs_2_, f32[4,6,256]{2,1,0:T(8,128)S(1)} %collective-permute-done.3.refs_2_, f32[512,32]{1,0:T(8,128)S(1)} %shard_map.30.refs_3_), custom_call_target="tpu_custom_call" | custom-call | flops 9961472 | tf_op jit(solution)/shard_map/pallas_call | solution.py:158
  12.9 0.0 collective-permute-done.2.refs_2_
  12.9 1.5 %collective-permute-start.4 = (f32[8,6,256]{2,1,0:T(8,128)S(1)}, f32[8,6,256]{2,1,0:T(8,128)S(1)}, u32[]{:S(2)}, u32[]{:S(2)}) collective-permute-start(f32[8,6,256]{2,1,0:T(8,128)S(1)} %pad_maximum_fusion), channel_id=1, source_target_pairs={{0,3},{1,2},{2,1},{3,0},{4,7},{5,6},{6,5},{7,4},{8,11},{9,10},{10,... | collective-permute-start | bytes 147464 | tf_op jit(solution)/shard_map/ppermute | solution.py:175
  14.4 0.2 collective-permute-start.5
  14.6 1.2 %shard_map.32.refs_3_ = f32[512,32]{1,0:T(8,128)S(1)} custom-call(f32[3,256,128]{2,1,0:T(8,128)S(1)} %get-tuple-element.22.refs_0_.refs_1_, bf16[256,48]{1,0:T(8,128)(2,1)S(1)} %get-tuple-element.23.refs_1_.refs_2_, f32[4,6,256]{2,1,0:T(8,128)S(1)} %collective-permute-done.2.refs_2_, f32[512,32]{1,0:T(8,128)S(1)} %shard_map.31.refs_3_), custom_call_target="tpu_custom_call" | custom-call | flops 9961472 | tf_op jit(solution)/shard_map/pallas_call | solution.py:158
  15.8 0.0 collective-permute-done.5.refs_2_
  15.8 1.2 %shard_map.33.refs_3_ = f32[512,32]{1,0:T(8,128)S(1)} custom-call(f32[3,256,128]{2,1,0:T(8,128)S(1)} %get-tuple-element.22.refs_0_.refs_1_, bf16[256,48]{1,0:T(8,128)(2,1)S(1)} %get-tuple-element.23.refs_1_.refs_2_, f32[4,6,256]{2,1,0:T(8,128)S(1)} %collective-permute-done.5.refs_2_, f32[512,32]{1,0:T(8,128)S(1)} %shard_map.32.refs_3_), custom_call_target="tpu_custom_call" | custom-call | flops 9961472 | tf_op jit(solution)/shard_map/pallas_call | solution.py:158
  17.1 0.0 collective-permute-done.4.refs_2_
  17.1 0.4 %collective-permute-start.6 = (f32[8,6,256]{2,1,0:T(8,128)S(1)}, f32[8,6,256]{2,1,0:T(8,128)S(1)}, u32[]{:S(2)}, u32[]{:S(2)}) collective-permute-start(f32[8,6,256]{2,1,0:T(8,128)S(1)} %collective-permute-done.4.refs_2_), channel_id=1, source_target_pairs={{0,1},{1,0},{2,3},{3,2},{4,5},{5,4},{6,7},{7,6},{8,9},{9,8},{10,11... | collective-permute-start | bytes 147464 | tf_op jit(solution)/shard_map/ppermute | solution.py:175
  17.4 2.3 %shard_map.34.refs_4_ = f32[512,32]{1,0:T(8,128)S(1)} custom-call(f32[3,256,128]{2,1,0:T(8,128)S(1)} %get-tuple-element.22.refs_0_.refs_1_, bf16[256,48]{1,0:T(8,128)(2,1)S(1)} %get-tuple-element.23.refs_1_.refs_2_, f32[8,6,256]{2,1,0:T(8,128)S(1)} %collective-permute-done.4.refs_2_, f32[512,32]{1,0:T(8,128)S(1)} %shard_map.33.refs_3_), custom_call_target="tpu_custom_call" | custom-call | flops 19922944 | tf_op jit(solution)/shard_map/pallas_call | solution.py:158
  19.7 0.0 collective-permute-done.6.refs_3_
  19.8 2.9 %shard_map.35 = f32[3,256]{1,0:T(4,128)} custom-call(f32[6,256]{1,0:T(8,128)S(1)} %get-tuple-element.40.refs_0_, f32[3,256,128]{2,1,0:T(8,128)S(1)} %get-tuple-element.22.refs_0_.refs_1_, bf16[256,48]{1,0:T(8,128)(2,1)S(1)} %get-tuple-element.23.refs_1_.refs_2_, f32[8,6,256]{2,1,0:T(8,128)S(1)} %collective-permute-done.6.refs_3_, ...), custom_call_target="tpu_custom_call" | custom-call | flops 19922944 | tf_op jit(solution)/shard_map/pallas_call | solution.py:158
  (4 shorter events, 0.0 us)
Async XLA Ops:
  0.0 0.7 %copy-start = (f32[3,256]{1,0:T(4,128)S(1)}, f32[3,256]{1,0:T(4,128)}, u32[]{:S(2)}) copy-start(f32[3,256]{1,0:T(4,128)} %param.3) | copy-start | bytes 9220
  0.7 4.9 %collective-permute-start = (f32[1,6,256]{2,1,0:T(8,128)S(1)}, f32[1,6,256]{2,1,0:T(8,128)S(1)}, u32[]{:S(2)}, u32[]{:S(2)}) collective-permute-start(f32[1,6,256]{2,1,0:T(8,128)S(1)} %get-tuple-element.39.refs_1_), channel_id=1, source_target_pairs={{0,17},{1,16},{2,19},{3,18},{4,21},{5,20},{6,23},{7,22},{8,25},{9,... | collective-permute-start | bytes 18440 | tf_op jit(solution)/shard_map/ppermute | solution.py:175
  5.6 3.3 %collective-permute-start.1 = (f32[2,6,256]{2,1,0:T(8,128)S(1)}, f32[2,6,256]{2,1,0:T(8,128)S(1)}, u32[]{:S(2)}, u32[]{:S(2)}) collective-permute-start(f32[2,6,256]{2,1,0:T(8,128)S(1)} %pad_maximum_fusion.2), channel_id=1, source_target_pairs={{0,9},{1,8},{2,11},{3,10},{4,13},{5,12},{6,15},{7,14},{8,1},{9,0},... | collective-permute-start | bytes 36872 | tf_op jit(solution)/shard_map/ppermute | solution.py:175
  9.0 2.7 %collective-permute-start.3 = (f32[4,6,256]{2,1,0:T(8,128)S(1)}, f32[4,6,256]{2,1,0:T(8,128)S(1)}, u32[]{:S(2)}, u32[]{:S(2)}) collective-permute-start(f32[4,6,256]{2,1,0:T(8,128)S(1)} %pad_maximum_fusion.1), channel_id=1, source_target_pairs={{0,1},{1,0},{2,3},{3,2},{4,5},{5,4},{6,7},{7,6},{8,9},{9,8},{10,11... | collective-permute-start | bytes 73736 | tf_op jit(solution)/shard_map/ppermute | solution.py:175
  9.4 3.5 %collective-permute-start.2 = (f32[4,6,256]{2,1,0:T(8,128)S(1)}, f32[4,6,256]{2,1,0:T(8,128)S(1)}, u32[]{:S(2)}, u32[]{:S(2)}) collective-permute-start(f32[4,6,256]{2,1,0:T(8,128)S(1)} %pad_maximum_fusion.1), channel_id=1, source_target_pairs={{0,5},{1,4},{2,7},{3,6},{4,1},{5,0},{6,3},{7,2},{8,13},{9,12},{10,... | collective-permute-start | bytes 73736 | tf_op jit(solution)/shard_map/ppermute | solution.py:175
  12.9 4.1 %collective-permute-start.4 = (f32[8,6,256]{2,1,0:T(8,128)S(1)}, f32[8,6,256]{2,1,0:T(8,128)S(1)}, u32[]{:S(2)}, u32[]{:S(2)}) collective-permute-start(f32[8,6,256]{2,1,0:T(8,128)S(1)} %pad_maximum_fusion), channel_id=1, source_target_pairs={{0,3},{1,2},{2,1},{3,0},{4,7},{5,6},{6,5},{7,4},{8,11},{9,10},{10,... | collective-permute-start | bytes 147464 | tf_op jit(solution)/shard_map/ppermute | solution.py:175
  14.4 1.4 %collective-permute-start.5 = (f32[4,6,256]{2,1,0:T(8,128)S(1)}, f32[4,6,256]{2,1,0:T(8,128)S(1)}, u32[]{:S(2)}, u32[]{:S(2)}) collective-permute-start(f32[4,6,256]{2,1,0:T(8,128)S(1)} %collective-permute-done.2.refs_2_), channel_id=1, source_target_pairs={{0,1},{1,0},{2,3},{3,2},{4,5},{5,4},{6,7},{7,6},{8,9},{9,8},{10,11... | collective-permute-start | bytes 73736 | tf_op jit(solution)/shard_map/ppermute | solution.py:175
  17.1 2.7 %collective-permute-start.6 = (f32[8,6,256]{2,1,0:T(8,128)S(1)}, f32[8,6,256]{2,1,0:T(8,128)S(1)}, u32[]{:S(2)}, u32[]{:S(2)}) collective-permute-start(f32[8,6,256]{2,1,0:T(8,128)S(1)} %collective-permute-done.4.refs_2_), channel_id=1, source_target_pairs={{0,1},{1,0},{2,3},{3,2},{4,5},{5,4},{6,7},{7,6},{8,9},{9,8},{10,11... | collective-permute-start | bytes 147464 | tf_op jit(solution)/shard_map/ppermute | solution.py:175

commit v6 on v5

--- a/solution.py
+++ b/solution.py
@@ -192,8 +192,8 @@
         known = len(bits) - step - 1
         if known == 1:
             across = swap(held, 1)
-        state = accumulate(own, state, [fresh])
-        if known < 2:
+        state = accumulate(own, state, [fresh, across] if known == 1 else [fresh])
+        if known == 0:
             across, state = after(across, state)
             state = accumulate(own, state, [across])
         got, state = after(got, state)

time: 22.9 us -> 22.9 us (level)
    pallas_call x8 -> x7, Pallas kernels: 10.6 us -> 10.5 us  [accumulate(): pl.pallas_call(functools.partial(kernel, len(sources), first, last), out_...]
  transfers between devices with their start and end apart: 7 -> 7, of which waited for: 2 -> 3; matrix products, arithmetic and copies ran while one was open for 0% -> 0% of each run, Pallas kernels for 34% -> 33%
where the time goes in v6:
time: 22.9 us; the launch traced here: 22.7 us
  Pallas kernels  10.5 us (46%)
  starting transfers between devices  9.54 us (42%)
  waiting for transfers between devices  1.87 us (8%)
  other arithmetic  0.73 us (3%)
    pallas_call x7, Pallas kernels, accumulate(): pl.pallas_call(functools.partial(kernel, len(sources), first, last), out_...  10.5 us
    ppermute x7, starting transfers between devices, swap(): return lax.ppermute(block, AXES, [(i, i ^ bit) for i in range(devices)])  9.54 us
    ppermute x7, waiting for transfers between devices, swap(): return lax.ppermute(block, AXES, [(i, i ^ bit) for i in range(devices)])  1.87 us
    mul x1, other arithmetic, body(): block = jnp.concatenate([1.5 * positions, forces], axis=0)[None]  0.7 us
  transfers between devices with their start and end apart: 7, of which 3 were waited for; matrix products, arithmetic and copies ran while one was open for 0% of the time, Pallas kernels for 33%

profile of v6, /device:TPU:0, one launch (start us, length us, event | category | flops | bytes accessed | tf_op | source)
XLA Modules:
  0.0 22.7 jit_solution(5096711926590544862)
XLA Ops:
  0.0 0.0 copy-start
  0.0 0.7 %broadcast_multiply_fusion = f32[3,256]{1,0:T(4,128)S(1)} fusion(f32[3,256]{1,0:T(4,128)} %param.2), kind=kLoop, calls=%fused_computation.4 | loop fusion | flops 768 | bytes 6144 | tf_op jit(solution)/shard_map/mul | solution.py:187
  0.7 0.0 copy-done
  0.7 3.5 %collective-permute-start = (f32[1,6,256]{2,1,0:T(8,128)S(1)}, f32[1,6,256]{2,1,0:T(8,128)S(1)}, u32[]{:S(2)}, u32[]{:S(2)}) collective-permute-start(f32[1,6,256]{2,1,0:T(8,128)S(1)} %get-tuple-element.35.refs_1_), channel_id=1, source_target_pairs={{0,17},{1,16},{2,19},{3,18},{4,21},{5,20},{6,23},{7,22},{8,25},{9,... | collective-permute-start | bytes 18440 | tf_op jit(solution)/shard_map/ppermute | solution.py:175
  4.3 0.7 %shard_map.28 = (f32[3,256,128]{2,1,0:T(8,128)S(1)}, bf16[256,48]{1,0:T(8,128)(2,1)S(1)}, f32[512,32]{1,0:T(8,128)S(1)}) custom-call(f32[6,256]{1,0:T(8,128)S(1)} %get-tuple-element.36.refs_0_, f32[1,6,256]{2,1,0:T(8,128)S(1)} %get-tuple-element.35.refs_1_), custom_call_target="tpu_custom_call" | custom-call | flops 2490368 | tf_op jit(solution)/shard_map/pallas_call | solution.py:158
  5.0 0.7 %collective-permute-done.refs_2_ = f32[1,6,256]{2,1,0:T(8,128)S(1)} collective-permute-done((f32[1,6,256]{2,1,0:T(8,128)S(1)}, f32[1,6,256]{2,1,0:T(8,128)S(1)}, u32[]{:S(2)}, u32[]{:S(2)}) %collective-permute-start) | collective-permute-done | bytes 6176 | tf_op jit(solution)/shard_map/ppermute | solution.py:175
  5.6 1.9 %collective-permute-start.1 = (f32[2,6,256]{2,1,0:T(8,128)S(1)}, f32[2,6,256]{2,1,0:T(8,128)S(1)}, u32[]{:S(2)}, u32[]{:S(2)}) collective-permute-start(f32[2,6,256]{2,1,0:T(8,128)S(1)} %pad_maximum_fusion.2), channel_id=1, source_target_pairs={{0,9},{1,8},{2,11},{3,10},{4,13},{5,12},{6,15},{7,14},{8,1},{9,0},... | collective-permute-start | bytes 36872 | tf_op jit(solution)/shard_map/ppermute | solution.py:175
  7.5 0.4 %shard_map.29.refs_4_ = f32[512,32]{1,0:T(8,128)S(1)} custom-call(f32[3,256,128]{2,1,0:T(8,128)S(1)} %get-tuple-element.20.refs_0_.refs_1_, bf16[256,48]{1,0:T(8,128)(2,1)S(1)} %get-tuple-element.21.refs_1_.refs_2_, f32[1,6,256]{2,1,0:T(8,128)S(1)} %collective-permute-done.refs_2_, f32[512,32]{1,0:T(8,128)S(1)} %get-tuple-element.24.refs_3_), custom_call_target="tpu_custom_call" | custom-call | flops 2490368 | tf_op jit(solution)/shard_map/pallas_call | solution.py:158
  7.9 1.0 %collective-permute-done.1.refs_2_ = f32[2,6,256]{2,1,0:T(8,128)S(1)} collective-permute-done((f32[2,6,256]{2,1,0:T(8,128)S(1)}, f32[2,6,256]{2,1,0:T(8,128)S(1)}, u32[]{:S(2)}, u32[]{:S(2)}) %collective-permute-start.1) | collective-permute-done | bytes 12320 | tf_op jit(solution)/shard_map/ppermute | solution.py:175
  9.0 0.5 %collective-permute-start.3 = (f32[4,6,256]{2,1,0:T(8,128)S(1)}, f32[4,6,256]{2,1,0:T(8,128)S(1)}, u32[]{:S(2)}, u32[]{:S(2)}) collective-permute-start(f32[4,6,256]{2,1,0:T(8,128)S(1)} %pad_maximum_fusion.1), channel_id=1, source_target_pairs={{0,1},{1,0},{2,3},{3,2},{4,5},{5,4},{6,7},{7,6},{8,9},{9,8},{10,11... | collective-permute-start | bytes 73736 | tf_op jit(solution)/shard_map/ppermute | solution.py:175
  9.4 1.5 %collective-permute-start.2 = (f32[4,6,256]{2,1,0:T(8,128)S(1)}, f32[4,6,256]{2,1,0:T(8,128)S(1)}, u32[]{:S(2)}, u32[]{:S(2)}) collective-permute-start(f32[4,6,256]{2,1,0:T(8,128)S(1)} %pad_maximum_fusion.1), channel_id=1, source_target_pairs={{0,5},{1,4},{2,7},{3,6},{4,1},{5,0},{6,3},{7,2},{8,13},{9,12},{10,... | collective-permute-start | bytes 73736 | tf_op jit(solution)/shard_map/ppermute | solution.py:175
  11.0 0.0 collective-permute-done.3.refs_3_
  11.0 1.8 %shard_map.30.refs_3_ = f32[512,32]{1,0:T(8,128)S(1)} custom-call(f32[3,256,128]{2,1,0:T(8,128)S(1)} %get-tuple-element.20.refs_0_.refs_1_, bf16[256,48]{1,0:T(8,128)(2,1)S(1)} %get-tuple-element.21.refs_1_.refs_2_, f32[2,6,256]{2,1,0:T(8,128)S(1)} %collective-permute-done.1.refs_2_, f32[4,6,256]{2,1,0:T(8,128)S(1)} %collective-permute-done.3.refs_3_, ...), custom_call_target="tpu_custom_call" | custom-call | flops 14942208 | tf_op jit(solution)/shard_map/pallas_call | solution.py:158
  12.8 0.1 collective-permute-done.2.refs_2_
  12.9 1.5 %collective-permute-start.4 = (f32[8,6,256]{2,1,0:T(8,128)S(1)}, f32[8,6,256]{2,1,0:T(8,128)S(1)}, u32[]{:S(2)}, u32[]{:S(2)}) collective-permute-start(f32[8,6,256]{2,1,0:T(8,128)S(1)} %pad_maximum_fusion), channel_id=1, source_target_pairs={{0,3},{1,2},{2,1},{3,0},{4,7},{5,6},{6,5},{7,4},{8,11},{9,10},{10,... | collective-permute-start | bytes 147464 | tf_op jit(solution)/shard_map/ppermute | solution.py:175
  14.4 0.2 collective-permute-start.5
  14.6 1.2 %shard_map.31.refs_3_ = f32[512,32]{1,0:T(8,128)S(1)} custom-call(f32[3,256,128]{2,1,0:T(8,128)S(1)} %get-tuple-element.20.refs_0_.refs_1_, bf16[256,48]{1,0:T(8,128)(2,1)S(1)} %get-tuple-element.21.refs_1_.refs_2_, f32[4,6,256]{2,1,0:T(8,128)S(1)} %collective-permute-done.2.refs_2_, f32[512,32]{1,0:T(8,128)S(1)} %shard_map.30.refs_3_), custom_call_target="tpu_custom_call" | custom-call | flops 9961472 | tf_op jit(solution)/shard_map/pallas_call | solution.py:158
  15.8 0.0 collective-permute-done.5.refs_2_
  15.8 1.2 %shard_map.32.refs_3_ = f32[512,32]{1,0:T(8,128)S(1)} custom-call(f32[3,256,128]{2,1,0:T(8,128)S(1)} %get-tuple-element.20.refs_0_.refs_1_, bf16[256,48]{1,0:T(8,128)(2,1)S(1)} %get-tuple-element.21.refs_1_.refs_2_, f32[4,6,256]{2,1,0:T(8,128)S(1)} %collective-permute-done.5.refs_2_, f32[512,32]{1,0:T(8,128)S(1)} %shard_map.31.refs_3_), custom_call_target="tpu_custom_call" | custom-call | flops 9961472 | tf_op jit(solution)/shard_map/pallas_call | solution.py:158
  17.0 0.0 collective-permute-done.4.refs_2_
  17.1 0.4 %collective-permute-start.6 = (f32[8,6,256]{2,1,0:T(8,128)S(1)}, f32[8,6,256]{2,1,0:T(8,128)S(1)}, u32[]{:S(2)}, u32[]{:S(2)}) collective-permute-start(f32[8,6,256]{2,1,0:T(8,128)S(1)} %collective-permute-done.4.refs_2_), channel_id=1, source_target_pairs={{0,1},{1,0},{2,3},{3,2},{4,5},{5,4},{6,7},{7,6},{8,9},{9,8},{10,11... | collective-permute-start | bytes 147464 | tf_op jit(solution)/shard_map/ppermute | solution.py:175
  17.4 2.3 %shard_map.33.refs_4_ = f32[512,32]{1,0:T(8,128)S(1)} custom-call(f32[3,256,128]{2,1,0:T(8,128)S(1)} %get-tuple-element.20.refs_0_.refs_1_, bf16[256,48]{1,0:T(8,128)(2,1)S(1)} %get-tuple-element.21.refs_1_.refs_2_, f32[8,6,256]{2,1,0:T(8,128)S(1)} %collective-permute-done.4.refs_2_, f32[512,32]{1,0:T(8,128)S(1)} %shard_map.32.refs_3_), custom_call_target="tpu_custom_call" | custom-call | flops 19922944 | tf_op jit(solution)/shard_map/pallas_call | solution.py:158
  19.7 0.0 collective-permute-done.6.refs_3_
  19.8 2.9 %shard_map.34 = f32[3,256]{1,0:T(4,128)} custom-call(f32[6,256]{1,0:T(8,128)S(1)} %get-tuple-element.36.refs_0_, f32[3,256,128]{2,1,0:T(8,128)S(1)} %get-tuple-element.20.refs_0_.refs_1_, bf16[256,48]{1,0:T(8,128)(2,1)S(1)} %get-tuple-element.21.refs_1_.refs_2_, f32[8,6,256]{2,1,0:T(8,128)S(1)} %collective-permute-done.6.refs_3_, ...), custom_call_target="tpu_custom_call" | custom-call | flops 19922944 | tf_op jit(solution)/shard_map/pallas_call | solution.py:158
  (4 shorter events, 0.0 us)
Async XLA Ops:
  0.0 0.7 %copy-start = (f32[3,256]{1,0:T(4,128)S(1)}, f32[3,256]{1,0:T(4,128)}, u32[]{:S(2)}) copy-start(f32[3,256]{1,0:T(4,128)} %param.3) | copy-start | bytes 9220
  0.7 4.9 %collective-permute-start = (f32[1,6,256]{2,1,0:T(8,128)S(1)}, f32[1,6,256]{2,1,0:T(8,128)S(1)}, u32[]{:S(2)}, u32[]{:S(2)}) collective-permute-start(f32[1,6,256]{2,1,0:T(8,128)S(1)} %get-tuple-element.35.refs_1_), channel_id=1, source_target_pairs={{0,17},{1,16},{2,19},{3,18},{4,21},{5,20},{6,23},{7,22},{8,25},{9,... | collective-permute-start | bytes 18440 | tf_op jit(solution)/shard_map/ppermute | solution.py:175
  5.6 3.3 %collective-permute-start.1 = (f32[2,6,256]{2,1,0:T(8,128)S(1)}, f32[2,6,256]{2,1,0:T(8,128)S(1)}, u32[]{:S(2)}, u32[]{:S(2)}) collective-permute-start(f32[2,6,256]{2,1,0:T(8,128)S(1)} %pad_maximum_fusion.2), channel_id=1, source_target_pairs={{0,9},{1,8},{2,11},{3,10},{4,13},{5,12},{6,15},{7,14},{8,1},{9,0},... | collective-permute-start | bytes 36872 | tf_op jit(solution)/shard_map/ppermute | solution.py:175
  9.0 2.0 %collective-permute-start.3 = (f32[4,6,256]{2,1,0:T(8,128)S(1)}, f32[4,6,256]{2,1,0:T(8,128)S(1)}, u32[]{:S(2)}, u32[]{:S(2)}) collective-permute-start(f32[4,6,256]{2,1,0:T(8,128)S(1)} %pad_maximum_fusion.1), channel_id=1, source_target_pairs={{0,1},{1,0},{2,3},{3,2},{4,5},{5,4},{6,7},{7,6},{8,9},{9,8},{10,11... | collective-permute-start | bytes 73736 | tf_op jit(solution)/shard_map/ppermute | solution.py:175
  9.4 3.4 %collective-permute-start.2 = (f32[4,6,256]{2,1,0:T(8,128)S(1)}, f32[4,6,256]{2,1,0:T(8,128)S(1)}, u32[]{:S(2)}, u32[]{:S(2)}) collective-permute-start(f32[4,6,256]{2,1,0:T(8,128)S(1)} %pad_maximum_fusion.1), channel_id=1, source_target_pairs={{0,5},{1,4},{2,7},{3,6},{4,1},{5,0},{6,3},{7,2},{8,13},{9,12},{10,... | collective-permute-start | bytes 73736 | tf_op jit(solution)/shard_map/ppermute | solution.py:175
  12.9 4.2 %collective-permute-start.4 = (f32[8,6,256]{2,1,0:T(8,128)S(1)}, f32[8,6,256]{2,1,0:T(8,128)S(1)}, u32[]{:S(2)}, u32[]{:S(2)}) collective-permute-start(f32[8,6,256]{2,1,0:T(8,128)S(1)} %pad_maximum_fusion), channel_id=1, source_target_pairs={{0,3},{1,2},{2,1},{3,0},{4,7},{5,6},{6,5},{7,4},{8,11},{9,10},{10,... | collective-permute-start | bytes 147464 | tf_op jit(solution)/shard_map/ppermute | solution.py:175
  14.4 1.4 %collective-permute-start.5 = (f32[4,6,256]{2,1,0:T(8,128)S(1)}, f32[4,6,256]{2,1,0:T(8,128)S(1)}, u32[]{:S(2)}, u32[]{:S(2)}) collective-permute-start(f32[4,6,256]{2,1,0:T(8,128)S(1)} %collective-permute-done.2.refs_2_), channel_id=1, source_target_pairs={{0,1},{1,0},{2,3},{3,2},{4,5},{5,4},{6,7},{7,6},{8,9},{9,8},{10,11... | collective-permute-start | bytes 73736 | tf_op jit(solution)/shard_map/ppermute | solution.py:175
  17.1 2.7 %collective-permute-start.6 = (f32[8,6,256]{2,1,0:T(8,128)S(1)}, f32[8,6,256]{2,1,0:T(8,128)S(1)}, u32[]{:S(2)}, u32[]{:S(2)}) collective-permute-start(f32[8,6,256]{2,1,0:T(8,128)S(1)} %collective-permute-done.4.refs_2_), channel_id=1, source_target_pairs={{0,1},{1,0},{2,3},{3,2},{4,5},{5,4},{6,7},{7,6},{8,9},{9,8},{10,11... | collective-permute-start | bytes 147464 | tf_op jit(solution)/shard_map/ppermute | solution.py:175
